TPU v7x, 32 devices: a whole 2x2x4 slice. The times are simulated.
32 devices in a mesh: px: 16 (over z, y, x), py: 2 (over core).
Axes of the slice: x: 2, y: 2, z: 4, core: 2. Of those that a mesh axis runs over, the one named last changes fastest.
Arguments:
- levels: int32 [256, 2048], P('px', 'py'), may hold values from 0 to 15
- conv_table: bfloat16 [64, 144], replicated, may hold values from -2 to 2
- conv_bias: float32 [64], replicated, may hold values from -3 to 3
- mix_weight: bfloat16 [64, 64], replicated, may hold values from -0.75 to 0.75
- mix_bias: float32 [64], replicated, may hold values from -3 to 3
- decoder: bfloat16 [5, 40, 64], replicated, may hold values from -0.15625 to 0.15625
- green_rows: float32 [8, 2, 64, 256], P(None, None, None, 'px'), may hold values from -0.375 to 0.375
- green_cols: float32 [8, 2, 64, 2048], P(None, None, None, 'py'), may hold values from -0.125 to 0.125
- focal_order: int32 [64], replicated, may hold values from 0 to 63, each once
Outputs:
- focal: float32 [8, 64, 512], P('py', 'px')
Inputs may be any that keep to these rules, and one draw needn't show every extreme that they name: `focal_order`: each of the 64 focal rows appears exactly once.
All inputs are finite; a program needn't handle non-finite values.
Results may differ from a plain program's by a relative error of at most 0.0045.
Values sent between devices are 32-bit elements; how exact they have to be, the bound alone decides.
A program may use at most 128 MiB of HBM per device.

v0:
```python
import functools

import jax
import jax.numpy as jnp
from jax import lax
from jax.experimental import pallas as pl
from jax.experimental.pallas import tpu as pltpu
from jax.sharding import PartitionSpec as P

CH = 8
M = 2
KS = 5
Z = 8
U = 64
V = 64
LEVELS = 16
HID = 64
LANE = 128
MESH = pl.DeviceIdType.MESH
F32 = jnp.float32
BF16 = jnp.bfloat16


def gelu(x):
    inner = x * (0.7978845608028654 + (0.7978845608028654 * 0.044715) * (x * x))
    half = 0.5 * x
    return half + half * jnp.tanh(inner)


def column(row):
    n = row.shape[1]
    here = lax.broadcasted_iota(jnp.int32, (n, n), 0) == lax.broadcasted_iota(jnp.int32, (n, n), 1)
    return jnp.sum(jnp.where(here, row, 0.0), axis=1, keepdims=True)


def nt_dot(a, b):
    return lax.dot_general(a, b, (((1,), (1,)), ((), ())), preferred_element_type=F32)


def kernel(
    npx, npy, scatter,
    lv, table, conv_bias, mix, mix_bias, dec, rows_in, cols_in, order, out,
    lvx, lv_right, lv_left, lvr, onehot, w1, w2, wd, taps, cols, cols_right, cols_left, colsb,
    rows_up, rows_down, lhs, rhs, field, r0, a0, r1a, r1b, a1a, a1b, r2a, r2b, a2, r3,
    send, recv, rs_send, rs_recv, load_sem,
):
    px = lax.axis_index("px")
    py = lax.axis_index("py")
    ncols = lv.shape[1]
    wide = ncols + LANE
    nrows = lv.shape[0]
    ext = nrows + 2 * M

    up, down = lax.rem(px + npx - 1, npx), lax.rem(px + 1, npx)
    left, right = lax.rem(py + npy - 1, npy), lax.rem(py + 1, npy)
    near = [(up, py), (down, py), (px, left), (px, right), (up, left), (up, right), (down, left), (down, right)]
    greeted = list(near)
    if scatter:
        xq = lax.rem(px, 2)
        yq = lax.rem(px // 2, 2)
        zq = px // 4
        xdev = (px + 1 - 2 * xq, py)
        ydev = (px + 2 - 4 * yq, py)
        zdevs = [(lax.rem(px + 4 * d, 16), py) for d in (1, 2, 3)]
        greeted += [xdev, ydev] + zdevs

    load = pltpu.make_async_copy(cols_in, cols, load_sem)
    load.start()
    barrier = pltpu.get_barrier_semaphore()
    for device in greeted:
        pl.semaphore_signal(barrier, inc=1, device_id=device, device_id_type=MESH)

    w1[...] = jnp.zeros_like(w1)
    for r in range(2):
        w1[HID * r : HID * (r + 1), 48 * r : 48 * r + 144] = table[...].astype(F32)
    w2[...] = jnp.zeros_like(w2)
    for r in range(4):
        w2[HID * r : HID * (r + 1), HID * r : HID * (r + 1)] = mix[...].astype(F32)
    wd[...] = jnp.zeros_like(wd)
    for r in range(4):
        for t in range(KS):
            e = r + t
            wd[40 * e : 40 * (e + 1), HID * r : HID * (r + 1)] = dec[t].astype(F32)
    w1b = w1[...].astype(BF16)
    w2b = w2[...].astype(BF16)
    wdb = wd[...].astype(BF16)
    bias1 = column(conv_bias[...])
    bias1 = jnp.concatenate([bias1, bias1], axis=0)
    bias2 = column(mix_bias[...])
    bias2 = jnp.concatenate([bias2] * 4, axis=0)

    pl.semaphore_wait(barrier, len(greeted))

    def remote(slot, src, dst, device):
        copy = pltpu.make_async_remote_copy(
            src_ref=src, dst_ref=dst, send_sem=send.at[slot], recv_sem=recv.at[slot],
            device_id=device, device_id_type=MESH,
        )
        copy.start()
        return copy

    last = ncols - LANE
    level_copies = [
        remote(0, lv.at[nrows - 8 : nrows, :], lvx.at[0:8, :], (down, py)),
        remote(1, lv.at[0:8, :], lvx.at[8:16, :], (up, py)),
        remote(2, lv.at[:, 0:LANE], lv_right.at[8:24, :], (px, left)),
        remote(3, lv.at[:, last:ncols], lv_left.at[8:24, :], (px, right)),
        remote(4, lv.at[nrows - 8 : nrows, 0:LANE], lv_right.at[0:8, :], (down, left)),
        remote(5, lv.at[nrows - 8 : nrows, last:ncols], lv_left.at[0:8, :], (down, right)),
        remote(6, lv.at[0:8, 0:LANE], lv_right.at[24:32, :], (up, left)),
        remote(7, lv.at[0:8, last:ncols], lv_left.at[24:32, :], (up, right)),
    ]
    green_copies = [
        remote(8, rows_in, rows_up, (down, py)),
        remote(9, rows_in, rows_down, (up, py)),
        remote(10, cols_in.at[:, 0:LANE], cols_right, (px, left)),
        remote(11, cols_in.at[:, last:ncols], cols_left, (px, right)),
    ]
    for copy in level_copies:
        copy.wait()

    first_up, last_down = px == 0, px == npx - 1
    first_left, last_right = py == 0, py == npy - 1
    lane = lax.broadcasted_iota(jnp.int32, (32, LANE), 1)
    sub = lax.broadcasted_iota(jnp.int32, (32, LANE), 0)
    side = jnp.where(
        lane < 64,
        jnp.where(last_right, -1, lv_right[...]),
        jnp.where(first_left, -1, lv_left[...]),
    )
    side = jnp.where((sub < 8) & first_up, -1, side)
    side = jnp.where((sub >= 24) & last_down, -1, side)
    body = jnp.concatenate(
        [
            jnp.where(first_up, -1, lvx[0:8, :]),
            lv[...],
            jnp.where(last_down, -1, lvx[8:16, :]),
        ],
        axis=0,
    )
    whole = jnp.concatenate([body, side], axis=1)
    lvr[0] = pltpu.roll(whole, 1, 1)[:, :ncols]
    lvr[1] = body
    lvr[2] = pltpu.roll(whole, wide - 1, 1)[:, :ncols]
    ids = lax.broadcasted_iota(jnp.int32, (LEVELS, ncols), 0)
    for i in range(nrows + 2):
        for b in range(3):
            row = lvr[b, 7 + i : 8 + i, :]
            match = jnp.where(ids == row, 1.0, 0.0).astype(BF16)
            onehot[(3 * i + b) * LEVELS : (3 * i + b + 1) * LEVELS, :] = match

    for g in range(nrows // 4):
        parts = []
        for r in range(2):
            first = 96 * (2 * g + r)
            act = jnp.dot(w1b, onehot[first : first + 192, :], preferred_element_type=F32) + bias1
            parts.append(gelu(act).astype(BF16))
        hidden = jnp.concatenate(parts, axis=0)
        act = jnp.dot(w2b, hidden, preferred_element_type=F32) + bias2
        features = gelu(act).astype(BF16)
        tap = jnp.dot(wdb, features, preferred_element_type=F32)
        at = 160 * g
        if g == 0:
            taps[0:320, :] = tap
        else:
            taps[at : at + 160, :] += tap[0:160]
            taps[at + 160 : at + 320, :] = tap[160:320]

    blank = jnp.zeros((CH, LANE), F32)
    tiles = []
    for e in range(ext):
        total = None
        for s in range(KS):
            piece = jnp.concatenate([taps[40 * e + 8 * s : 40 * e + 8 * s + 8, :], blank], axis=1)
            if s != M:
                piece = pltpu.roll(piece, (s - M) % wide, 1)
            total = piece if total is None else total + piece
        tiles.append(total)
    near_field = jnp.concatenate(tiles, axis=0).astype(BF16)
    pr = lax.broadcasted_iota(jnp.int32, (CH * 32, CH * ext), 0)
    pc = lax.broadcasted_iota(jnp.int32, (CH * 32, CH * ext), 1)
    perm = jnp.where((pr // 32 == pc % 8) & ((pc // 8 + 30) % 32 == pr % 32), 1.0, 0.0).astype(BF16)
    near_field = jnp.dot(perm, near_field, preferred_element_type=F32).astype(BF16)

    for copy in green_copies:
        copy.wait()
    load.wait()
    colsb[:, 0:ncols] = cols[...].astype(BF16)
    clane = lax.broadcasted_iota(jnp.int32, cols_right.shape, 1)
    colsb[:, ncols:wide] = jnp.where(
        clane < 64,
        jnp.where(last_right, 0.0, cols_right[...]),
        jnp.where(first_left, 0.0, cols_left[...]),
    ).astype(BF16)

    share = U // npx
    height = U * Z
    er = lax.broadcasted_iota(jnp.int32, (height, U), 0)
    ec = lax.broadcasted_iota(jnp.int32, (height, U), 1)
    pick = jnp.where((er // (share * Z)) * share + er % share == ec, 1.0, 0.0).astype(BF16)
    wr = lax.broadcasted_iota(jnp.int32, (U, U), 0)
    placed = jnp.where(wr == order[...], 1.0, 0.0).astype(BF16)
    pick = nt_dot(pick, placed).astype(BF16)
    rlane = lax.broadcasted_iota(jnp.int32, rows_in.shape, 1)
    mixed = jnp.where(
        rlane % 16 < 8,
        jnp.where(last_down, 0.0, rows_down[...]),
        jnp.where(first_up, 0.0, rows_up[...]),
    )
    zr = (lax.broadcasted_iota(jnp.int32, (height, 256), 0) // share) % Z
    zc = lax.broadcasted_iota(jnp.int32, (height, 256), 1) // 32
    for source, value in enumerate((rows_in[...], mixed)):
        chosen = jnp.dot(pick, value.astype(BF16), preferred_element_type=F32)
        lhs[:, 256 * source : 256 * (source + 1)] = jnp.where(zr == zc, chosen, 0.0).astype(BF16)

    sums = nt_dot(near_field, colsb[...])
    sign = jnp.where(lax.broadcasted_iota(jnp.int32, (32, LANE), 1) < 64, -1.0, 1.0)
    for z in range(Z):
        for p in range(CH // 2):
            one = sums[32 * p : 32 * p + 32, LANE * z : LANE * (z + 1)]
            two = sums[32 * p + 128 : 32 * p + 160, LANE * z : LANE * (z + 1)]
            first = (one + sign * pltpu.roll(two, 64, 1)).astype(BF16)
            second = (sign * pltpu.roll(one, 64, 1) - two).astype(BF16)
            at = slice(LANE * p, LANE * (p + 1))
            for source in range(2):
                base = 256 * source + 32 * z
                rhs[base : base + 16, at] = first[16 * source : 16 * source + 16]
                rhs[base + 16 : base + 32, at] = second[16 * source : 16 * source + 16]
    product = jnp.dot(lhs[...], rhs[...], preferred_element_type=F32)
    if not scatter:
        out[...] = product
        return

    field[...] = product.reshape(field.shape)

    def exchange(slot, src, dst, device):
        copy = pltpu.make_async_remote_copy(
            src_ref=src, dst_ref=dst, send_sem=rs_send.at[slot], recv_sem=rs_recv.at[slot],
            device_id=device, device_id_type=MESH,
        )
        copy.start()
        return copy

    mine = pl.multiple_of(py * 16, 16)
    other = pl.multiple_of((1 - py) * 16, 16)
    core = exchange(0, field.at[:, :, :, pl.ds(other, 16), :], r0, (px, 1 - py))
    core.wait()
    a0[...] = field[:, :, :, pl.ds(mine, 16), :] + r0[...]
    half = a0.shape[-1] // 2
    ca = exchange(1, a0.at[:, :, 1 - xq, :, 0:half], r1a, xdev)
    cb = exchange(2, a0.at[:, 1 - yq, :, :, half : 2 * half], r1b, ydev)
    ca.wait()
    a1a[...] = a0[:, :, xq, :, 0:half] + r1a[...]
    da = exchange(3, a1a.at[:, 1 - yq], r2a, ydev)
    cb.wait()
    a1b[...] = a0[:, yq, :, :, half : 2 * half] + r1b[...]
    db = exchange(4, a1b.at[:, 1 - xq], r2b, xdev)
    da.wait()
    a2[:, :, 0:half] = a1a[:, yq] + r2a[...]
    db.wait()
    a2[:, :, half : 2 * half] = a1b[:, xq] + r2b[...]
    last_copies = [
        exchange(5 + d, a2.at[lax.rem(zq + d + 1, 4)], r3.at[d], zdevs[d]) for d in range(3)
    ]
    result = a2[zq]
    for d, copy in enumerate(last_copies):
        copy.wait()
        result = result + r3[d]
    low = lax.broadcasted_iota(jnp.int32, (16, LANE), 1) < 64
    reals, imags = [], []
    for j in range(2):
        even = result[:, 2 * j * LANE : (2 * j + 1) * LANE]
        odd = result[:, (2 * j + 1) * LANE : (2 * j + 2) * LANE]
        reals.append(jnp.where(low, even, pltpu.roll(odd, 64, 1)))
        imags.append(jnp.where(low, pltpu.roll(even, 64, 1), odd))
    out[...] = jnp.concatenate(reals + imags, axis=1)


def on_device(
    levels, conv_table, conv_bias, mix_weight, mix_bias, decoder, green_rows, green_cols, focal_order
):
    npx = lax.axis_size("px")
    npy = lax.axis_size("py")
    nrows, ncols = levels.shape
    wide = ncols + LANE
    scatter = npx == 16 and npy == 2
    width = CH * V
    height = U * Z
    rows = green_rows.transpose(2, 0, 1, 3).reshape(U, Z * 2 * nrows)
    cols = green_cols.reshape(Z * 2 * V, ncols)
    out_rows = 16 if scatter else height
    vmem = pl.BlockSpec(memory_space=pltpu.VMEM)
    half = width // 2
    rs = (lambda *shape: pltpu.VMEM(shape, F32)) if scatter else (lambda *shape: pltpu.VMEM((8, LANE), F32))
    result = pl.pallas_call(
        functools.partial(kernel, npx, npy, scatter),
        out_shape=jax.ShapeDtypeStruct((out_rows, width), F32),
        in_specs=[vmem] * 7 + [pl.BlockSpec(memory_space=pl.ANY), vmem],
        out_specs=vmem,
        scratch_shapes=[
            pltpu.VMEM((16, ncols), jnp.int32),
            pltpu.VMEM((32, LANE), jnp.int32),
            pltpu.VMEM((32, LANE), jnp.int32),
            pltpu.VMEM((3, 32, ncols), jnp.int32),
            pltpu.VMEM(((nrows + 2) * 3 * LEVELS, ncols), BF16),
            pltpu.VMEM((2 * HID, 192), F32),
            pltpu.VMEM((4 * HID, 4 * HID), F32),
            pltpu.VMEM((8 * KS * CH, 4 * HID), F32),
            pltpu.VMEM(((nrows + 2 * M) * KS * CH, ncols), F32),
            pltpu.VMEM(cols.shape, F32),
            pltpu.VMEM((cols.shape[0], LANE), F32),
            pltpu.VMEM((cols.shape[0], LANE), F32),
            pltpu.VMEM((cols.shape[0], wide), BF16),
            pltpu.VMEM(rows.shape, F32),
            pltpu.VMEM(rows.shape, F32),
            pltpu.VMEM((height, 512), BF16),
            pltpu.VMEM((512, width), BF16),
            rs(4, 2, 2, 32, width),
            rs(4, 2, 2, 16, width),
            rs(4, 2, 2, 16, width),
            rs(4, 2, 16, half),
            rs(4, 2, 16, half),
            rs(4, 2, 16, half),
            rs(4, 2, 16, half),
            rs(4, 16, half),
            rs(4, 16, half),
            rs(4, 16, width),
            rs(3, 16, width),
            pltpu.SemaphoreType.DMA((12,)),
            pltpu.SemaphoreType.DMA((12,)),
            pltpu.SemaphoreType.DMA((8,)),
            pltpu.SemaphoreType.DMA((8,)),
            pltpu.SemaphoreType.DMA,
        ],
        compiler_params=pltpu.CompilerParams(
            collective_id=0, has_side_effects=True, vmem_limit_bytes=48 * 1024 * 1024
        ),
    )(
        levels, conv_table, conv_bias.reshape(1, HID), mix_weight, mix_bias.reshape(1, HID),
        decoder, rows, cols, focal_order.reshape(1, U),
    )
    if scatter:
        return result.reshape(Z // npy, U // npx, width)
    own = lax.psum_scatter(result, ("px", "py"), scatter_dimension=0, tiled=True)
    own = own.reshape(Z // npy, U // npx, CH // 2, 2, V).transpose(0, 1, 3, 2, 4)
    return own.reshape(Z // npy, U // npx, width)


def solution(mesh):
    return jax.shard_map(
        on_device,
        mesh=mesh,
        in_specs=(
            P("px", "py"),
            P(),
            P(),
            P(),
            P(),
            P(),
            P(None, None, None, "px"),
            P(None, None, None, "py"),
            P(),
        ),
        out_specs=P("py", "px", None),
        check_vma=False,
    )
```

profile of v0, /device:TPU:0, one launch (start us, length us, event | category | flops | bytes accessed | tf_op | source)
XLA Modules:
  0.0 41.9 jit_solution(5738532185424536081)
XLA Ops:
  0.0 1.0 %copy.11.rows_in = f32[64,256]{1,0:T(8,128)S(1)} copy(f32[64,256]{0,1:T(8,128)} %bitcast.11) | data formatting | bytes 131072 | tf_op jit(solution)/shard_map/reshape | solution.py:289
  1.0 0.0 copy-start
  1.0 2.2 %copy-done = f32[8,2,64,1024]{3,2,1,0:T(8,128)S(1)} copy-done((f32[8,2,64,1024]{3,2,1,0:T(8,128)S(1)}, f32[8,2,64,1024]{3,2,1,0:T(8,128)}, u32[]{:S(2)}) %copy-start) | copy-done | bytes 4194328
  3.2 0.0 copy-start.1
  3.2 0.8 %copy-done.1 = s32[16,1024]{1,0:T(8,128)S(1)} copy-done((s32[16,1024]{1,0:T(8,128)S(1)}, s32[16,1024]{1,0:T(8,128)}, u32[]{:S(2)}) %copy-start.1) | copy-done | bytes 65560
  4.0 0.0 copy-start.2
  4.0 0.8 %copy-done.2 = bf16[5,40,64]{2,1,0:T(8,128)(2,1)S(1)} copy-done((bf16[5,40,64]{2,1,0:T(8,128)(2,1)S(1)}, bf16[5,40,64]{2,1,0:T(8,128)(2,1)}, u32[]{:S(2)}) %copy-start.2) | copy-done | bytes 25624
  4.8 0.0 copy-start.3
  4.8 0.8 %copy-done.3 = bf16[64,144]{1,0:T(8,128)(2,1)S(1)} copy-done((bf16[64,144]{1,0:T(8,128)(2,1)S(1)}, bf16[64,144]{1,0:T(8,128)(2,1)}, u32[]{:S(2)}) %copy-start.3) | copy-done | bytes 18456
  5.6 0.0 copy-start.4
  5.6 0.7 %copy-done.4 = bf16[64,64]{1,0:T(8,128)(2,1)S(1)} copy-done((bf16[64,64]{1,0:T(8,128)(2,1)S(1)}, bf16[64,64]{1,0:T(8,128)(2,1)}, u32[]{:S(2)}) %copy-start.4) | copy-done | bytes 8216
  6.3 0.0 copy-start.5
  6.3 0.7 %copy-done.5 = f32[64]{0:T(128)S(1)} copy-done((f32[64]{0:T(128)S(1)}, f32[64]{0:T(128)}, u32[]{:S(2)}) %copy-start.5) | copy-done | bytes 280
  7.0 0.0 copy-start.6
  7.0 0.7 %copy-done.6 = f32[64]{0:T(128)S(1)} copy-done((f32[64]{0:T(128)S(1)}, f32[64]{0:T(128)}, u32[]{:S(2)}) %copy-start.6) | copy-done | bytes 280
  7.6 0.0 copy-start.7
  7.6 0.7 %copy-done.7 = s32[64]{0:T(128)S(1)} copy-done((s32[64]{0:T(128)S(1)}, s32[64]{0:T(128)}, u32[]{:S(2)}) %copy-start.7) | copy-done | bytes 280
  8.3 33.0 %shard_map.91 = f32[16,512]{1,0:T(8,128)S(1)} custom-call(s32[16,1024]{1,0:T(8,128)S(1)} %copy-done.1, bf16[64,144]{1,0:T(8,128)(2,1)S(1)} %copy-done.3, f32[1,64]{1,0:T(1,128)S(1)} %bitcast.8, bf16[64,64]{1,0:T(8,128)(2,1)S(1)} %copy-done.4, f32[1,64]{1,0:T(1,128)S(1)} %bitcast.9, bf16[5,40,64]{2,1,0:T(8,128)(2,1)S(1)} %copy-done.2, ...), custom_call_target="tpu_custom_call" | custom-call | tf_op jit(solution)/shard_map/pallas_call | solution.py:295
  41.3 0.6 %reshape.23 = f32[4,4,512]{2,1,0:T(4,128)} reshape(f32[16,512]{1,0:T(8,128)S(1)} %shard_map.91) | data formatting | bytes 65536 | tf_op jit(solution)/shard_map/reshape | solution.py:343
Async XLA Ops:
  1.0 2.2 %copy-start = (f32[8,2,64,1024]{3,2,1,0:T(8,128)S(1)}, f32[8,2,64,1024]{3,2,1,0:T(8,128)}, u32[]{:S(2)}) copy-start(f32[8,2,64,1024]{3,2,1,0:T(8,128)} %param.16) | copy-start | bytes 12582916
  3.2 0.8 %copy-start.1 = (s32[16,1024]{1,0:T(8,128)S(1)}, s32[16,1024]{1,0:T(8,128)}, u32[]{:S(2)}) copy-start(s32[16,1024]{1,0:T(8,128)} %lv.1) | copy-start | bytes 196612
  4.0 0.8 %copy-start.2 = (bf16[5,40,64]{2,1,0:T(8,128)(2,1)S(1)}, bf16[5,40,64]{2,1,0:T(8,128)(2,1)}, u32[]{:S(2)}) copy-start(bf16[5,40,64]{2,1,0:T(8,128)(2,1)} %dec.1) | copy-start | bytes 76804
  4.8 0.8 %copy-start.3 = (bf16[64,144]{1,0:T(8,128)(2,1)S(1)}, bf16[64,144]{1,0:T(8,128)(2,1)}, u32[]{:S(2)}) copy-start(bf16[64,144]{1,0:T(8,128)(2,1)} %table.1) | copy-start | bytes 55300
  5.6 0.7 %copy-start.4 = (bf16[64,64]{1,0:T(8,128)(2,1)S(1)}, bf16[64,64]{1,0:T(8,128)(2,1)}, u32[]{:S(2)}) copy-start(bf16[64,64]{1,0:T(8,128)(2,1)} %mix.1) | copy-start | bytes 24580
  6.3 0.7 %copy-start.5 = (f32[64]{0:T(128)S(1)}, f32[64]{0:T(128)}, u32[]{:S(2)}) copy-start(f32[64]{0:T(128)} %param.11) | copy-start | bytes 772
  7.0 0.7 %copy-start.6 = (f32[64]{0:T(128)S(1)}, f32[64]{0:T(128)}, u32[]{:S(2)}) copy-start(f32[64]{0:T(128)} %param.13) | copy-start | bytes 772
  7.6 0.7 %copy-start.7 = (s32[64]{0:T(128)S(1)}, s32[64]{0:T(128)}, u32[]{:S(2)}) copy-start(s32[64]{0:T(128)} %param.17) | copy-start | bytes 772
where the time goes:
time: 42.3 us; the launch traced here: 41.9 us
  Pallas kernels  33 us (78%)
  local copies, waits for them, and re-layouts  8.87 us (21%)
    pallas_call x1, Pallas kernels, on_device(): pl.pallas_call(functools.partial(kernel, npx, npy, scatter), out_shape=ja...  33 us
    unnamed x16, local copies, waits for them, and re-layouts  7.26 us
    reshape x1, local copies, waits for them, and re-layouts, on_device(): rows = green_rows.transpose(2, 0, 1, 3).reshape(U, Z * 2 * nrows)  0.98 us

commit v1 on v0

v1 whole, which is shorter than its diff:
```python
import functools

import jax
import jax.numpy as jnp
from jax import lax
from jax.experimental import pallas as pl
from jax.experimental.pallas import tpu as pltpu
from jax.sharding import PartitionSpec as P

CH = 8
M = 2
KS = 5
Z = 8
U = 64
V = 64
LEVELS = 16
HID = 64
LANE = 128
MESH = pl.DeviceIdType.MESH
F32 = jnp.float32
BF16 = jnp.bfloat16


def gelu(half):
    inner = half * (1.5957691216057308 + (1.5957691216057308 * 4 * 0.044715) * (half * half))
    return half + half * jnp.tanh(inner)


def column(row):
    n = row.shape[1]
    here = lax.broadcasted_iota(jnp.int32, (n, n), 0) == lax.broadcasted_iota(jnp.int32, (n, n), 1)
    return jnp.sum(jnp.where(here, row, 0.0), axis=1, keepdims=True)


def nt_dot(a, b):
    return lax.dot_general(a, b, (((1,), (1,)), ((), ())), preferred_element_type=F32)


def kernel(
    npx, npy, scatter,
    lv_in, table_in, cb_in, mix_in, mb_in, dec_in, rows_in, cols_in, order_in, out,
    lv, table, conv_bias, mix, mix_bias, dec, rows, order,
    lvx, lv_right, lv_left, lvr, onehot, w1, w2, wd, taps, cols, cols_right, cols_left, colsb,
    rows_up, rows_down, lhs, rhs, field, r0, a0, r1a, r1b, a1a, a1b, r2a, r2b, a2, r3,
    send, recv, rs_send, rs_recv, load_sem,
):
    px = lax.axis_index("px")
    py = lax.axis_index("py")
    nrows, ncols = lv.shape
    wide = ncols + LANE
    ext = nrows + 2 * M

    up, down = lax.rem(px + npx - 1, npx), lax.rem(px + 1, npx)
    left, right = lax.rem(py + npy - 1, npy), lax.rem(py + 1, npy)
    greeted = [
        (up, py), (down, py), (px, left), (px, right),
        (up, left), (up, right), (down, left), (down, right),
    ]
    if scatter:
        xq = lax.rem(px, 2)
        yq = lax.rem(px // 2, 2)
        zq = px // 4
        xdev = (px + 1 - 2 * xq, py)
        ydev = (px + 2 - 4 * yq, py)
        zdevs = [(lax.rem(px + 4 * d, 16), py) for d in (1, 2, 3)]
        greeted += [xdev, ydev] + zdevs

    barrier = pltpu.get_barrier_semaphore()
    for device in greeted:
        pl.semaphore_signal(barrier, inc=1, device_id=device, device_id_type=MESH)
    loads = []
    for i, (src, dst) in enumerate([
        (table_in, table), (cb_in, conv_bias), (mix_in, mix), (mb_in, mix_bias), (dec_in, dec),
        (lv_in, lv), (rows_in, rows), (order_in, order), (cols_in, cols),
    ]):
        loads.append(pltpu.make_async_copy(src, dst, load_sem.at[i]))
        loads[-1].start()
    for load in loads[:5]:
        load.wait()

    w1[...] = jnp.zeros_like(w1)
    for r in range(2):
        w1[HID * r : HID * (r + 1), 48 * r : 48 * r + 144] = 0.5 * table[...].astype(F32)
    w2[...] = jnp.zeros_like(w2)
    for r in range(4):
        w2[HID * r : HID * (r + 1), HID * r : HID * (r + 1)] = 0.5 * mix[...].astype(F32)
    wd[...] = jnp.zeros_like(wd)
    for r in range(4):
        for t in range(KS):
            e = r + t
            wd[40 * e : 40 * (e + 1), HID * r : HID * (r + 1)] = dec[t].astype(F32)
    w1b = w1[...].astype(BF16)
    w2b = w2[...].astype(BF16)
    wdb = wd[...].astype(BF16)
    bias1 = column(0.5 * conv_bias[...])
    bias1 = jnp.concatenate([bias1, bias1], axis=0)
    bias2 = column(0.5 * mix_bias[...])
    bias2 = jnp.concatenate([bias2] * 4, axis=0)

    pl.semaphore_wait(barrier, len(greeted))

    def remote(slot, src, dst, device):
        copy = pltpu.make_async_remote_copy(
            src_ref=src, dst_ref=dst, send_sem=send.at[slot], recv_sem=recv.at[slot],
            device_id=device, device_id_type=MESH,
        )
        copy.start()
        return copy

    last = ncols - LANE
    side_copies = [
        remote(0, lv_in.at[:, 0:LANE], lv_right.at[8:24, :], (px, left)),
        remote(1, lv_in.at[:, last:ncols], lv_left.at[8:24, :], (px, right)),
    ]
    edge_copies = [
        remote(2, lv_in.at[nrows - 8 : nrows, :], lvx.at[0:8, :], (down, py)),
        remote(3, lv_in.at[0:8, :], lvx.at[8:16, :], (up, py)),
        remote(4, lv_in.at[nrows - 8 : nrows, 0:LANE], lv_right.at[0:8, :], (down, left)),
        remote(5, lv_in.at[nrows - 8 : nrows, last:ncols], lv_left.at[0:8, :], (down, right)),
        remote(6, lv_in.at[0:8, 0:LANE], lv_right.at[24:32, :], (up, left)),
        remote(7, lv_in.at[0:8, last:ncols], lv_left.at[24:32, :], (up, right)),
    ]
    green_copies = [
        remote(8, rows_in, rows_up, (down, py)),
        remote(9, rows_in, rows_down, (up, py)),
        remote(10, cols_in.at[:, 0:LANE], cols_right, (px, left)),
        remote(11, cols_in.at[:, last:ncols], cols_left, (px, right)),
    ]
    for load in loads[5:]:
        load.wait()
    colsb[:, 0:ncols] = cols[...].astype(BF16)

    first_up, last_down = px == 0, px == npx - 1
    first_left, last_right = py == 0, py == npy - 1
    ids = lax.broadcasted_iota(jnp.int32, (LEVELS, ncols), 0)

    def place(at, body, outside):
        n = body.shape[0]
        lane = lax.broadcasted_iota(jnp.int32, (n, LANE), 1)
        side = jnp.where(
            lane < 64,
            jnp.where(last_right, -1, lv_right[at : at + n, :]),
            jnp.where(first_left, -1, lv_left[at : at + n, :]),
        )
        whole = jnp.concatenate([body, side], axis=1)
        if outside is not None:
            whole = jnp.where(outside, -1, whole)
        lvr[0, at : at + n, :] = pltpu.roll(whole, 1, 1)[:, :ncols]
        lvr[1, at : at + n, :] = whole[:, :ncols]
        lvr[2, at : at + n, :] = pltpu.roll(whole, wide - 1, 1)[:, :ncols]

    def encode(i):
        for b in range(3):
            row = lvr[b, 7 + i : 8 + i, :]
            match = jnp.where(ids == row, 1.0, 0.0).astype(BF16)
            onehot[(3 * i + b) * LEVELS : (3 * i + b + 1) * LEVELS, :] = match

    def group(g):
        parts = []
        for r in range(2):
            first = 96 * (2 * g + r)
            act = jnp.dot(w1b, onehot[first : first + 192, :], preferred_element_type=F32) + bias1
            parts.append(gelu(act).astype(BF16))
        hidden = jnp.concatenate(parts, axis=0)
        act = jnp.dot(w2b, hidden, preferred_element_type=F32) + bias2
        features = gelu(act).astype(BF16)
        return jnp.dot(wdb, features, preferred_element_type=F32)

    for copy in side_copies:
        copy.wait()
    place(8, lv[...], None)
    for i in range(1, nrows + 1):
        encode(i)
    tap = group(1)
    taps[160:480, :] = tap
    tap = group(2)
    taps[320:480, :] += tap[0:160]
    taps[480:640, :] = tap[160:320]
    for copy in edge_copies:
        copy.wait()
    place(0, lvx[0:8, :], first_up)
    place(24, lvx[8:16, :], last_down)
    encode(0)
    encode(nrows + 1)
    tap = group(0)
    taps[0:160, :] = tap[0:160]
    taps[160:320, :] += tap[160:320]
    tap = group(3)
    taps[480:640, :] += tap[0:160]
    taps[640:800, :] = tap[160:320]

    for copy in green_copies:
        copy.wait()
    clane = lax.broadcasted_iota(jnp.int32, cols_right.shape, 1)
    colsb[:, ncols:wide] = jnp.where(
        clane < 64,
        jnp.where(last_right, 0.0, cols_right[...]),
        jnp.where(first_left, 0.0, cols_left[...]),
    ).astype(BF16)

    share = U // npx
    er = lax.broadcasted_iota(jnp.int32, (2 * U, U), 0)
    ec = lax.broadcasted_iota(jnp.int32, (2 * U, U), 1)
    pick = jnp.where((er // (2 * share)) * share + er % share == ec, 1.0, 0.0).astype(BF16)
    wr = lax.broadcasted_iota(jnp.int32, (U, U), 0)
    placed = jnp.where(wr == order[...], 1.0, 0.0).astype(BF16)
    pick = nt_dot(pick, placed).astype(BF16)
    xrow = lax.broadcasted_iota(jnp.int32, rows.shape, 0) % 16
    mixed = jnp.where(
        xrow < 8,
        jnp.where(last_down, 0.0, rows_down[...]),
        jnp.where(first_up, 0.0, rows_up[...]),
    ).astype(BF16)
    own = rows[...].astype(BF16)
    zr = (lax.broadcasted_iota(jnp.int32, (2 * U, LANE), 0) // share) % 2
    zc = (lax.broadcasted_iota(jnp.int32, (2 * U, LANE), 1) // 32) % 2
    for c in range(Z // 2):
        both = jnp.concatenate([own[64 * c : 64 * c + 64], mixed[64 * c : 64 * c + 64]], axis=0)
        lhs[c] = jnp.where(zr == zc, nt_dot(pick, both), 0.0).astype(BF16)

    blank = jnp.zeros((CH, LANE), F32)
    tiles = []
    for e in range(ext):
        total = None
        for s in range(KS):
            piece = jnp.concatenate([taps[40 * e + 8 * s : 40 * e + 8 * s + 8, :], blank], axis=1)
            if s != M:
                piece = pltpu.roll(piece, (s - M) % wide, 1)
            total = piece if total is None else total + piece
        tiles.append(total)
    near_field = jnp.concatenate(tiles, axis=0).astype(BF16)
    pr = lax.broadcasted_iota(jnp.int32, (CH * 32, CH * ext), 0)
    pc = lax.broadcasted_iota(jnp.int32, (CH * 32, CH * ext), 1)
    perm = jnp.where((pr // 32 == pc % 8) & ((pc // 8 + 30) % 32 == pr % 32), 1.0, 0.0).astype(BF16)
    near_field = jnp.dot(perm, near_field, preferred_element_type=F32).astype(BF16)
    sign = jnp.where(lax.broadcasted_iota(jnp.int32, (32, LANE), 1) < 64, -1.0, 1.0)

    def planes(c, slot):
        cut = pl.ds(pl.multiple_of(256 * c, 256), 256)
        sums = nt_dot(near_field, colsb[cut, :])
        for z in range(2):
            for p in range(CH // 2):
                one = sums[32 * p : 32 * p + 32, LANE * z : LANE * (z + 1)]
                two = sums[32 * p + 128 : 32 * p + 160, LANE * z : LANE * (z + 1)]
                at = slice(LANE * p, LANE * (p + 1))
                for k, value in enumerate((
                    one + sign * pltpu.roll(two, 64, 1), sign * pltpu.roll(one, 64, 1) - two
                )):
                    high = value.astype(BF16)
                    low = (value - high.astype(F32)).astype(BF16)
                    for source in range(2):
                        base = 64 * source + 32 * z + 16 * k
                        rhs[slot, 0, base : base + 16, at] = high[16 * source : 16 * source + 16]
                        rhs[slot, 1, base : base + 16, at] = low[16 * source : 16 * source + 16]
        left_side = lhs[c]
        return jnp.dot(left_side, rhs[slot, 0], preferred_element_type=F32) + jnp.dot(
            left_side, rhs[slot, 1], preferred_element_type=F32
        )

    if not scatter:
        for c in range(Z // 2):
            out[c] = planes(c, c)
        return

    def exchange(slot, src, dst, device):
        copy = pltpu.make_async_remote_copy(
            src_ref=src, dst_ref=dst, send_sem=rs_send.at[slot], recv_sem=rs_recv.at[slot],
            device_id=device, device_id_type=MESH,
        )
        copy.start()
        return copy

    half = a0.shape[-1] // 2
    core = []
    for i in range(2):
        field[i] = planes(2 * (1 - py) + i, i).reshape(field.shape[1:])
        core.append(exchange(i, field.at[i], r0.at[i], (px, 1 - py)))
    step1 = []
    for i in range(2):
        value = planes(2 * py + i, 2 + i).reshape(field.shape[1:])
        core[i].wait()
        a0[i] = value + r0[i]
        step1.append((
            exchange(2 + 7 * i, a0.at[i, :, :, 1 - xq, :, 0:half], r1a.at[i], xdev),
            exchange(3 + 7 * i, a0.at[i, :, 1 - yq, :, :, half : 2 * half], r1b.at[i], ydev),
        ))
    step2 = []
    for i in range(2):
        step1[i][0].wait()
        a1a[i] = a0[i, :, :, xq, :, 0:half] + r1a[i]
        da = exchange(4 + 7 * i, a1a.at[i, :, 1 - yq], r2a.at[i], ydev)
        step1[i][1].wait()
        a1b[i] = a0[i, :, yq, :, :, half : 2 * half] + r1b[i]
        db = exchange(5 + 7 * i, a1b.at[i, :, 1 - xq], r2b.at[i], xdev)
        step2.append((da, db))
    step3 = []
    for i in range(2):
        step2[i][0].wait()
        a2[i, :, :, 0:half] = a1a[i, :, yq] + r2a[i]
        step2[i][1].wait()
        a2[i, :, :, half : 2 * half] = a1b[i, :, xq] + r2b[i]
        step3.append([
            exchange(6 + 7 * i + d, a2.at[i, lax.rem(zq + d + 1, 4)], r3.at[i, d], zdevs[d])
            for d in range(3)
        ])
    low = lax.broadcasted_iota(jnp.int32, (8, LANE), 1) < 64
    for i in range(2):
        result = a2[i, zq]
        for d, copy in enumerate(step3[i]):
            copy.wait()
            result = result + r3[i, d]
        reals, imags = [], []
        for j in range(2):
            even = result[:, 2 * j * LANE : (2 * j + 1) * LANE]
            odd = result[:, (2 * j + 1) * LANE : (2 * j + 2) * LANE]
            reals.append(jnp.where(low, even, pltpu.roll(odd, 64, 1)))
            imags.append(jnp.where(low, pltpu.roll(even, 64, 1), odd))
        out[8 * i : 8 * i + 8, :] = jnp.concatenate(reals + imags, axis=1)


def on_device(
    levels, conv_table, conv_bias, mix_weight, mix_bias, decoder, green_rows, green_cols, focal_order
):
    npx = lax.axis_size("px")
    npy = lax.axis_size("py")
    nrows, ncols = levels.shape
    wide = ncols + LANE
    scatter = npx == 16 and npy == 2
    width = CH * V
    share = U // npx
    rows = green_rows.transpose(0, 1, 3, 2).reshape(Z * 2 * nrows, U)
    cols = green_cols.reshape(Z * 2 * V, ncols)
    operands = (
        levels, conv_table, conv_bias.reshape(1, HID), mix_weight, mix_bias.reshape(1, HID),
        decoder, rows, cols, focal_order.reshape(1, U),
    )
    half = width // 2

    def rs(*shape):
        return pltpu.VMEM(shape if scatter else (8, LANE), F32)

    def like(array):
        return pltpu.VMEM(array.shape, array.dtype)

    result = pl.pallas_call(
        functools.partial(kernel, npx, npy, scatter),
        out_shape=jax.ShapeDtypeStruct((16, width) if scatter else (Z // 2, 2 * U, width), F32),
        in_specs=[pl.BlockSpec(memory_space=pltpu.HBM)] * 9,
        out_specs=pl.BlockSpec(memory_space=pltpu.VMEM),
        scratch_shapes=[
            *[like(operands[i]) for i in (0, 1, 2, 3, 4, 5, 6, 8)],
            pltpu.VMEM((16, ncols), jnp.int32),
            pltpu.VMEM((32, LANE), jnp.int32),
            pltpu.VMEM((32, LANE), jnp.int32),
            pltpu.VMEM((3, 32, ncols), jnp.int32),
            pltpu.VMEM(((nrows + 2) * 3 * LEVELS, ncols), BF16),
            pltpu.VMEM((2 * HID, 192), F32),
            pltpu.VMEM((4 * HID, 4 * HID), F32),
            pltpu.VMEM((8 * KS * CH, 4 * HID), F32),
            pltpu.VMEM(((nrows + 2 * M) * KS * CH, ncols), F32),
            pltpu.VMEM(cols.shape, F32),
            pltpu.VMEM((cols.shape[0], LANE), F32),
            pltpu.VMEM((cols.shape[0], LANE), F32),
            pltpu.VMEM((cols.shape[0], wide), BF16),
            like(rows),
            like(rows),
            pltpu.VMEM((Z // 2, 2 * U, LANE), BF16),
            pltpu.VMEM((4, 2, LANE, width), BF16),
            rs(2, 4, 2, 2, 8, width),
            rs(2, 4, 2, 2, 8, width),
            rs(2, 4, 2, 2, 8, width),
            rs(2, 4, 2, 8, half),
            rs(2, 4, 2, 8, half),
            rs(2, 4, 2, 8, half),
            rs(2, 4, 2, 8, half),
            rs(2, 4, 8, half),
            rs(2, 4, 8, half),
            rs(2, 4, 8, width),
            rs(2, 3, 8, width),
            pltpu.SemaphoreType.DMA((12,)),
            pltpu.SemaphoreType.DMA((12,)),
            pltpu.SemaphoreType.DMA((16,)),
            pltpu.SemaphoreType.DMA((16,)),
            pltpu.SemaphoreType.DMA((9,)),
        ],
        compiler_params=pltpu.CompilerParams(
            collective_id=0, has_side_effects=True, vmem_limit_bytes=56 * 1024 * 1024
        ),
    )(*operands)
    if scatter:
        return result.reshape(Z // npy, share, width)
    result = result.reshape(Z // 2, npx, 2, share, width).transpose(1, 0, 2, 3, 4)
    own = lax.psum_scatter(result.reshape(Z * U, width), ("px", "py"), scatter_dimension=0, tiled=True)
    own = own.reshape(Z // npy, share, CH // 2, 2, V).transpose(0, 1, 3, 2, 4)
    return own.reshape(Z // npy, share, width)


def solution(mesh):
    return jax.shard_map(
        on_device,
        mesh=mesh,
        in_specs=(
            P("px", "py"),
            P(),
            P(),
            P(),
            P(),
            P(),
            P(None, None, None, "px"),
            P(None, None, None, "py"),
            P(),
        ),
        out_specs=P("py", "px", None),
        check_vma=False,
    )
```

time: 42.3 us -> 32.4 us (0.77)
  local copies, waits for them, and re-layouts: 8.87 us -> 1.39 us
  Pallas kernels: 33 us -> 30.8 us
    unnamed x16 -> x0, local copies, waits for them, and re-layouts: 7.26 us -> none
    pallas_call x1, Pallas kernels: 33 us -> 30.8 us  [on_device(): pl.pallas_call(functools.partial(kernel, npx, npy, scatter), out_shape=ja...]
    reshape x2 -> x1, local copies, waits for them, and re-layouts: 1.61 us -> 1.39 us  [on_device(): return result.reshape(Z // npy, share, width)]
where the time goes in v1:
time: 32.4 us; the launch traced here: 32.2 us
  Pallas kernels  30.8 us (95%)
  local copies, waits for them, and re-layouts  1.39 us (4%)
    pallas_call x1, Pallas kernels, on_device(): pl.pallas_call(functools.partial(kernel, npx, npy, scatter), out_shape=ja...  30.8 us
    reshape x1, local copies, waits for them, and re-layouts, on_device(): return result.reshape(Z // npy, share, width)  1.39 us

profile of v1, /device:TPU:0, one launch (start us, length us, event | category | flops | bytes accessed | tf_op | source)
XLA Modules:
  0.0 32.2 jit_solution(13973463859249706919)
XLA Ops:
  0.0 30.8 %shard_map.91 = f32[16,512]{1,0:T(8,128)} custom-call(s32[16,1024]{1,0:T(8,128)} %lv_in.1, bf16[64,144]{1,0:T(8,128)(2,1)} %table_in.1, f32[1,64]{1,0:T(1,128)} %bitcast.9, bf16[64,64]{1,0:T(8,128)(2,1)} %mix_in.1, f32[1,64]{1,0:T(1,128)} %bitcast.10, bf16[5,40,64]{2,1,0:T(8,128)(2,1)} %dec_in.1, f32[256,64]{1,0:T(8,128)} %bitcast.8, f32[1024,1024]{1,0:T(8,128)} %bitcast.7, ...), custom_call_target="tpu_custom_call" | custom-call | tf_op jit(solution)/shard_map/pallas_call | solution.py:345
  30.8 1.4 %reshape.23 = f32[4,4,512]{2,1,0:T(4,128)} reshape(f32[16,512]{1,0:T(8,128)} %shard_map.91) | data formatting | bytes 65536 | tf_op jit(solution)/shard_map/reshape | solution.py:391

commit v2 on v1

--- a/solution.py
+++ b/solution.py
@@ -41,7 +41,7 @@
     lv_in, table_in, cb_in, mix_in, mb_in, dec_in, rows_in, cols_in, order_in, out,
     lv, table, conv_bias, mix, mix_bias, dec, rows, order,
     lvx, lv_right, lv_left, lvr, onehot, w1, w2, wd, taps, cols, cols_right, cols_left, colsb,
-    rows_up, rows_down, lhs, rhs, field, r0, a0, r1a, r1b, a1a, a1b, r2a, r2b, a2, r3,
+    rows_up, rows_down, lhs, field, r0, a0, r1a, r1b, a1a, a1b, r2a, r2b, a2, r3,
     send, recv, rs_send, rs_recv, load_sem,
 ):
     px = lax.axis_index("px")
@@ -129,6 +129,13 @@
     for load in loads[5:]:
         load.wait()
     colsb[:, 0:ncols] = cols[...].astype(BF16)
+    share = U // npx
+    er = lax.broadcasted_iota(jnp.int32, (4 * U, U), 0)
+    ec = lax.broadcasted_iota(jnp.int32, (4 * U, U), 1)
+    pick = jnp.where((er // (4 * share)) * share + er % share == ec, 1.0, 0.0).astype(BF16)
+    wr = lax.broadcasted_iota(jnp.int32, (U, U), 0)
+    placed = jnp.where(wr == order[...], 1.0, 0.0).astype(BF16)
+    pick = nt_dot(pick, placed).astype(BF16)
 
     first_up, last_down = px == 0, px == npx - 1
     first_left, last_right = py == 0, py == npy - 1
@@ -198,13 +205,6 @@
         jnp.where(first_left, 0.0, cols_left[...]),
     ).astype(BF16)
 
-    share = U // npx
-    er = lax.broadcasted_iota(jnp.int32, (2 * U, U), 0)
-    ec = lax.broadcasted_iota(jnp.int32, (2 * U, U), 1)
-    pick = jnp.where((er // (2 * share)) * share + er % share == ec, 1.0, 0.0).astype(BF16)
-    wr = lax.broadcasted_iota(jnp.int32, (U, U), 0)
-    placed = jnp.where(wr == order[...], 1.0, 0.0).astype(BF16)
-    pick = nt_dot(pick, placed).astype(BF16)
     xrow = lax.broadcasted_iota(jnp.int32, rows.shape, 0) % 16
     mixed = jnp.where(
         xrow < 8,
@@ -212,11 +212,15 @@
         jnp.where(first_up, 0.0, rows_up[...]),
     ).astype(BF16)
     own = rows[...].astype(BF16)
-    zr = (lax.broadcasted_iota(jnp.int32, (2 * U, LANE), 0) // share) % 2
-    zc = (lax.broadcasted_iota(jnp.int32, (2 * U, LANE), 1) // 32) % 2
-    for c in range(Z // 2):
-        both = jnp.concatenate([own[64 * c : 64 * c + 64], mixed[64 * c : 64 * c + 64]], axis=0)
-        lhs[c] = jnp.where(zr == zc, nt_dot(pick, both), 0.0).astype(BF16)
+    pr = (lax.broadcasted_iota(jnp.int32, (4 * U, 2 * LANE), 0) // share) % 4
+    pc = (lax.broadcasted_iota(jnp.int32, (4 * U, 2 * LANE), 1) // 32) % 4
+    for z in range(Z):
+        blocks = []
+        for k in range(2):
+            at = 32 * z + 16 * k
+            blocks += [own[at : at + 16], mixed[at : at + 16]] * 4
+        spread = nt_dot(pick, jnp.concatenate(blocks, axis=0))
+        lhs[z] = jnp.where(pr == pc, spread, 0.0).astype(BF16)
 
     blank = jnp.zeros((CH, LANE), F32)
     tiles = []
@@ -233,33 +237,28 @@
     pc = lax.broadcasted_iota(jnp.int32, (CH * 32, CH * ext), 1)
     perm = jnp.where((pr // 32 == pc % 8) & ((pc // 8 + 30) % 32 == pr % 32), 1.0, 0.0).astype(BF16)
     near_field = jnp.dot(perm, near_field, preferred_element_type=F32).astype(BF16)
-    sign = jnp.where(lax.broadcasted_iota(jnp.int32, (32, LANE), 1) < 64, -1.0, 1.0)
-
-    def planes(c, slot):
+
+    def planes(c):
         cut = pl.ds(pl.multiple_of(256 * c, 256), 256)
-        sums = nt_dot(near_field, colsb[cut, :])
+        sums = nt_dot(colsb[cut, :], near_field)
+        fields = []
         for z in range(2):
-            for p in range(CH // 2):
-                one = sums[32 * p : 32 * p + 32, LANE * z : LANE * (z + 1)]
-                two = sums[32 * p + 128 : 32 * p + 160, LANE * z : LANE * (z + 1)]
-                at = slice(LANE * p, LANE * (p + 1))
-                for k, value in enumerate((
-                    one + sign * pltpu.roll(two, 64, 1), sign * pltpu.roll(one, 64, 1) - two
-                )):
-                    high = value.astype(BF16)
-                    low = (value - high.astype(F32)).astype(BF16)
-                    for source in range(2):
-                        base = 64 * source + 32 * z + 16 * k
-                        rhs[slot, 0, base : base + 16, at] = high[16 * source : 16 * source + 16]
-                        rhs[slot, 1, base : base + 16, at] = low[16 * source : 16 * source + 16]
-        left_side = lhs[c]
-        return jnp.dot(left_side, rhs[slot, 0], preferred_element_type=F32) + jnp.dot(
-            left_side, rhs[slot, 1], preferred_element_type=F32
-        )
+            one = sums[LANE * z : LANE * z + LANE, 0:LANE]
+            two = sums[LANE * z : LANE * z + LANE, LANE : 2 * LANE]
+            real = one[0:64] - two[64:128]
+            imag = one[64:128] + two[0:64]
+            first = jnp.concatenate([real, imag], axis=0)
+            second = jnp.concatenate([-imag, real], axis=0)
+            value = jnp.concatenate([first, second], axis=1)
+            high = value.astype(BF16)
+            low = (value - high.astype(F32)).astype(BF16)
+            left_side = lhs[2 * c + z]
+            fields.append(nt_dot(left_side, high) + nt_dot(left_side, low))
+        return fields
 
     if not scatter:
         for c in range(Z // 2):
-            out[c] = planes(c, c)
+            out[2 * c], out[2 * c + 1] = planes(c)
         return
 
     def exchange(slot, src, dst, device):
@@ -270,52 +269,54 @@
         copy.start()
         return copy
 
-    half = a0.shape[-1] // 2
     core = []
     for i in range(2):
-        field[i] = planes(2 * (1 - py) + i, i).reshape(field.shape[1:])
+        for z, value in enumerate(planes(2 * (1 - py) + i)):
+            field[i, z] = value.reshape(field.shape[2:])
         core.append(exchange(i, field.at[i], r0.at[i], (px, 1 - py)))
     step1 = []
     for i in range(2):
-        value = planes(2 * py + i, 2 + i).reshape(field.shape[1:])
+        values = planes(2 * py + i)
         core[i].wait()
-        a0[i] = value + r0[i]
+        for z in range(2):
+            a0[i, z] = values[z].reshape(field.shape[2:]) + r0[i, z]
         step1.append((
-            exchange(2 + 7 * i, a0.at[i, :, :, 1 - xq, :, 0:half], r1a.at[i], xdev),
-            exchange(3 + 7 * i, a0.at[i, :, 1 - yq, :, :, half : 2 * half], r1b.at[i], ydev),
+            exchange(2 + 7 * i, a0.at[i, 0, :, :, 1 - xq], r1a.at[i], xdev),
+            exchange(3 + 7 * i, a0.at[i, 1, :, 1 - yq], r1b.at[i], ydev),
         ))
     step2 = []
     for i in range(2):
         step1[i][0].wait()
-        a1a[i] = a0[i, :, :, xq, :, 0:half] + r1a[i]
+        a1a[i] = a0[i, 0, :, :, xq] + r1a[i]
         da = exchange(4 + 7 * i, a1a.at[i, :, 1 - yq], r2a.at[i], ydev)
         step1[i][1].wait()
-        a1b[i] = a0[i, :, yq, :, :, half : 2 * half] + r1b[i]
+        a1b[i] = a0[i, 1, :, yq] + r1b[i]
         db = exchange(5 + 7 * i, a1b.at[i, :, 1 - xq], r2b.at[i], xdev)
         step2.append((da, db))
     step3 = []
     for i in range(2):
         step2[i][0].wait()
-        a2[i, :, :, 0:half] = a1a[i, :, yq] + r2a[i]
+        a2[i, :, 0] = a1a[i, :, yq] + r2a[i]
         step2[i][1].wait()
-        a2[i, :, :, half : 2 * half] = a1b[i, :, xq] + r2b[i]
+        a2[i, :, 1] = a1b[i, :, xq] + r2b[i]
         step3.append([
             exchange(6 + 7 * i + d, a2.at[i, lax.rem(zq + d + 1, 4)], r3.at[i, d], zdevs[d])
             for d in range(3)
         ])
-    low = lax.broadcasted_iota(jnp.int32, (8, LANE), 1) < 64
+    first_half = lax.broadcasted_iota(jnp.int32, (share, LANE), 1) < 64
     for i in range(2):
         result = a2[i, zq]
         for d, copy in enumerate(step3[i]):
             copy.wait()
             result = result + r3[i, d]
-        reals, imags = [], []
-        for j in range(2):
-            even = result[:, 2 * j * LANE : (2 * j + 1) * LANE]
-            odd = result[:, (2 * j + 1) * LANE : (2 * j + 2) * LANE]
-            reals.append(jnp.where(low, even, pltpu.roll(odd, 64, 1)))
-            imags.append(jnp.where(low, pltpu.roll(even, 64, 1), odd))
-        out[8 * i : 8 * i + 8, :] = jnp.concatenate(reals + imags, axis=1)
+        for z in range(2):
+            reals, imags = [], []
+            for j in range(2):
+                even = result[z, 2 * j * share : (2 * j + 1) * share]
+                odd = result[z, (2 * j + 1) * share : (2 * j + 2) * share]
+                reals.append(jnp.where(first_half, even, pltpu.roll(odd, 64, 1)))
+                imags.append(jnp.where(first_half, pltpu.roll(even, 64, 1), odd))
+            out[2 * i + z] = jnp.concatenate(reals + imags, axis=1)
 
 
 def on_device(
@@ -334,7 +335,6 @@
         levels, conv_table, conv_bias.reshape(1, HID), mix_weight, mix_bias.reshape(1, HID),
         decoder, rows, cols, focal_order.reshape(1, U),
     )
-    half = width // 2
 
     def rs(*shape):
         return pltpu.VMEM(shape if scatter else (8, LANE), F32)
@@ -344,7 +344,7 @@
 
     result = pl.pallas_call(
         functools.partial(kernel, npx, npy, scatter),
-        out_shape=jax.ShapeDtypeStruct((16, width) if scatter else (Z // 2, 2 * U, width), F32),
+        out_shape=jax.ShapeDtypeStruct((Z // npy, share, width) if scatter else (Z, 4 * U, 2 * V), F32),
         in_specs=[pl.BlockSpec(memory_space=pltpu.HBM)] * 9,
         out_specs=pl.BlockSpec(memory_space=pltpu.VMEM),
         scratch_shapes=[
@@ -364,19 +364,18 @@
             pltpu.VMEM((cols.shape[0], wide), BF16),
             like(rows),
             like(rows),
-            pltpu.VMEM((Z // 2, 2 * U, LANE), BF16),
-            pltpu.VMEM((4, 2, LANE, width), BF16),
-            rs(2, 4, 2, 2, 8, width),
-            rs(2, 4, 2, 2, 8, width),
-            rs(2, 4, 2, 2, 8, width),
-            rs(2, 4, 2, 8, half),
-            rs(2, 4, 2, 8, half),
-            rs(2, 4, 2, 8, half),
-            rs(2, 4, 2, 8, half),
-            rs(2, 4, 8, half),
-            rs(2, 4, 8, half),
-            rs(2, 4, 8, width),
-            rs(2, 3, 8, width),
+            pltpu.VMEM((Z, 4 * U, 2 * LANE), BF16),
+            rs(2, 2, 4, 2, 2, 16, LANE),
+            rs(2, 2, 4, 2, 2, 16, LANE),
+            rs(2, 2, 4, 2, 2, 16, LANE),
+            rs(2, 4, 2, 16, LANE),
+            rs(2, 4, 2, 16, LANE),
+            rs(2, 4, 2, 16, LANE),
+            rs(2, 4, 2, 16, LANE),
+            rs(2, 4, 16, LANE),
+            rs(2, 4, 16, LANE),
+            rs(2, 4, 2, 16, LANE),
+            rs(2, 3, 2, 16, LANE),
             pltpu.SemaphoreType.DMA((12,)),
             pltpu.SemaphoreType.DMA((12,)),
             pltpu.SemaphoreType.DMA((16,)),
@@ -388,10 +387,12 @@
         ),
     )(*operands)
     if scatter:
-        return result.reshape(Z // npy, share, width)
-    result = result.reshape(Z // 2, npx, 2, share, width).transpose(1, 0, 2, 3, 4)
-    own = lax.psum_scatter(result.reshape(Z * U, width), ("px", "py"), scatter_dimension=0, tiled=True)
-    own = own.reshape(Z // npy, share, CH // 2, 2, V).transpose(0, 1, 3, 2, 4)
+        return result
+    result = result.reshape(Z, npx, 4 * share, 2 * V).transpose(1, 0, 2, 3)
+    own = lax.psum_scatter(
+        result.reshape(npx * Z, 4 * share * 2 * V), ("px", "py"), scatter_dimension=0, tiled=True
+    )
+    own = own.reshape(Z // npy, CH // 2, share, 2, V).transpose(0, 2, 3, 1, 4)
     return own.reshape(Z // npy, share, width)
 
 

time: 32.4 us -> 32.4 us (level)
    reshape x1 -> x0, local copies, waits for them, and re-layouts: 1.39 us -> none  [on_device(): return result.reshape(Z // npy, share, width)]
    unnamed x0 -> x1, local copies, waits for them, and re-layouts: none -> 1.38 us
where the time goes in v2:
time: 32.4 us; the launch traced here: 32.2 us
  Pallas kernels  30.9 us (95%)
  local copies, waits for them, and re-layouts  1.38 us (4%)
    pallas_call x1, Pallas kernels, on_device(): pl.pallas_call(functools.partial(kernel, npx, npy, scatter), out_shape=ja...  30.9 us
    unnamed x1, local copies, waits for them, and re-layouts  1.38 us

profile of v2, /device:TPU:0, one launch (start us, length us, event | category | flops | bytes accessed | tf_op | source)
XLA Modules:
  0.0 32.2 jit_solution(8927309573058212285)
XLA Ops:
  0.0 30.9 %shard_map.91 = f32[4,4,512]{2,1,0:T(4,128)} custom-call(s32[16,1024]{1,0:T(8,128)} %lv_in.1, bf16[64,144]{1,0:T(8,128)(2,1)} %table_in.1, f32[1,64]{1,0:T(1,128)} %bitcast.9, bf16[64,64]{1,0:T(8,128)(2,1)} %mix_in.1, f32[1,64]{1,0:T(1,128)} %bitcast.10, bf16[5,40,64]{2,1,0:T(8,128)(2,1)} %dec_in.1, f32[256,64]{1,0:T(8,128)} %bitcast.8, ...), custom_call_target="tpu_custom_call" | custom-call | tf_op jit(solution)/shard_map/pallas_call | solution.py:345
  30.9 1.4 %copy.11 = f32[4,4,512]{2,1,0:T(4,128)} copy(f32[4,4,512]{2,1,0:T(4,128)} %shard_map.91) | data formatting | bytes 65536

commit v3 on v2

--- a/solution.py
+++ b/solution.py
@@ -40,7 +40,7 @@
     npx, npy, scatter,
     lv_in, table_in, cb_in, mix_in, mb_in, dec_in, rows_in, cols_in, order_in, out,
     lv, table, conv_bias, mix, mix_bias, dec, rows, order,
-    lvx, lv_right, lv_left, lvr, onehot, w1, w2, wd, taps, cols, cols_right, cols_left, colsb,
+    lvx, lv_right, lv_left, lvr, onehot, w1, w2, wd, biases, taps, cols, cols_right, cols_left, colsb,
     rows_up, rows_down, lhs, field, r0, a0, r1a, r1b, a1a, a1b, r2a, r2b, a2, r3,
     send, recv, rs_send, rs_recv, load_sem,
 ):
@@ -75,28 +75,6 @@
     ]):
         loads.append(pltpu.make_async_copy(src, dst, load_sem.at[i]))
         loads[-1].start()
-    for load in loads[:5]:
-        load.wait()
-
-    w1[...] = jnp.zeros_like(w1)
-    for r in range(2):
-        w1[HID * r : HID * (r + 1), 48 * r : 48 * r + 144] = 0.5 * table[...].astype(F32)
-    w2[...] = jnp.zeros_like(w2)
-    for r in range(4):
-        w2[HID * r : HID * (r + 1), HID * r : HID * (r + 1)] = 0.5 * mix[...].astype(F32)
-    wd[...] = jnp.zeros_like(wd)
-    for r in range(4):
-        for t in range(KS):
-            e = r + t
-            wd[40 * e : 40 * (e + 1), HID * r : HID * (r + 1)] = dec[t].astype(F32)
-    w1b = w1[...].astype(BF16)
-    w2b = w2[...].astype(BF16)
-    wdb = wd[...].astype(BF16)
-    bias1 = column(0.5 * conv_bias[...])
-    bias1 = jnp.concatenate([bias1, bias1], axis=0)
-    bias2 = column(0.5 * mix_bias[...])
-    bias2 = jnp.concatenate([bias2] * 4, axis=0)
-
     pl.semaphore_wait(barrier, len(greeted))
 
     def remote(slot, src, dst, device):
@@ -126,20 +104,36 @@
         remote(10, cols_in.at[:, 0:LANE], cols_right, (px, left)),
         remote(11, cols_in.at[:, last:ncols], cols_left, (px, right)),
     ]
-    for load in loads[5:]:
+    for load in loads[:5]:
         load.wait()
-    colsb[:, 0:ncols] = cols[...].astype(BF16)
-    share = U // npx
-    er = lax.broadcasted_iota(jnp.int32, (4 * U, U), 0)
-    ec = lax.broadcasted_iota(jnp.int32, (4 * U, U), 1)
-    pick = jnp.where((er // (4 * share)) * share + er % share == ec, 1.0, 0.0).astype(BF16)
-    wr = lax.broadcasted_iota(jnp.int32, (U, U), 0)
-    placed = jnp.where(wr == order[...], 1.0, 0.0).astype(BF16)
-    pick = nt_dot(pick, placed).astype(BF16)
+
+    w1[...] = jnp.zeros_like(w1)
+    for r in range(2):
+        w1[HID * r : HID * (r + 1), 48 * r : 48 * r + 144] = 0.5 * table[...].astype(F32)
+    w2[...] = jnp.zeros_like(w2)
+    for r in range(4):
+        w2[HID * r : HID * (r + 1), HID * r : HID * (r + 1)] = 0.5 * mix[...].astype(F32)
+    wd[...] = jnp.zeros_like(wd)
+    for r in range(4):
+        for t in range(KS):
+            e = r + t
+            wd[40 * e : 40 * (e + 1), HID * r : HID * (r + 1)] = dec[t].astype(F32)
+    w1b = w1[...].astype(BF16)
+    w2b = w2[...].astype(BF16)
+    wdb = wd[...].astype(BF16)
+    bias1 = jnp.broadcast_to(column(0.5 * conv_bias[...]), (HID, LANE))
+    bias2 = jnp.broadcast_to(column(0.5 * mix_bias[...]), (HID, LANE))
+    for r in range(2):
+        biases[HID * r : HID * (r + 1)] = bias1
+    for r in range(2, 6):
+        biases[HID * r : HID * (r + 1)] = bias2
 
     first_up, last_down = px == 0, px == npx - 1
     first_left, last_right = py == 0, py == npy - 1
-    ids = lax.broadcasted_iota(jnp.int32, (LEVELS, ncols), 0)
+    tile = 256
+    count = ncols // tile
+    inner, outer = range(1, count - 1), (0, count - 1)
+    ids = lax.broadcasted_iota(jnp.int32, (LEVELS, tile), 0)
 
     def place(at, body, outside):
         n = body.shape[0]
@@ -156,46 +150,75 @@
         lvr[1, at : at + n, :] = whole[:, :ncols]
         lvr[2, at : at + n, :] = pltpu.roll(whole, wide - 1, 1)[:, :ncols]
 
-    def encode(i):
+    def encode(i, t):
+        at = slice(tile * t, tile * (t + 1))
         for b in range(3):
-            row = lvr[b, 7 + i : 8 + i, :]
+            row = lvr[b, 7 + i : 8 + i, at]
             match = jnp.where(ids == row, 1.0, 0.0).astype(BF16)
-            onehot[(3 * i + b) * LEVELS : (3 * i + b + 1) * LEVELS, :] = match
-
-    def group(g):
+            onehot[(3 * i + b) * LEVELS : (3 * i + b + 1) * LEVELS, at] = match
+
+    def first_layer(g, t):
+        at = slice(tile * t, tile * (t + 1))
+        bias = jnp.concatenate([biases[0 : 2 * HID]] * 2, axis=1)
         parts = []
         for r in range(2):
             first = 96 * (2 * g + r)
-            act = jnp.dot(w1b, onehot[first : first + 192, :], preferred_element_type=F32) + bias1
+            act = jnp.dot(w1b, onehot[first : first + 192, at], preferred_element_type=F32) + bias
             parts.append(gelu(act).astype(BF16))
-        hidden = jnp.concatenate(parts, axis=0)
-        act = jnp.dot(w2b, hidden, preferred_element_type=F32) + bias2
-        features = gelu(act).astype(BF16)
-        return jnp.dot(wdb, features, preferred_element_type=F32)
+        return jnp.concatenate(parts, axis=0)
+
+    def second_layer(hidden):
+        bias = jnp.concatenate([biases[2 * HID : 6 * HID]] * 2, axis=1)
+        act = jnp.dot(w2b, hidden, preferred_element_type=F32) + bias
+        return gelu(act).astype(BF16)
+
+    def decode(g, t, features):
+        at = slice(tile * t, tile * (t + 1))
+        tap = jnp.dot(wdb, features, preferred_element_type=F32)
+        for part in range(2):
+            first = 160 * (g + part)
+            value = tap[160 * part : 160 * (part + 1)]
+            if (g, part) in ((1, 0), (1, 1), (2, 1), (0, 0), (3, 1)):
+                taps[first : first + 160, at] = value
+            else:
+                taps[first : first + 160, at] += value
+
+    def network(blocks):
+        hidden, features = {}, {}
+        for step in range(len(blocks) + 2):
+            if step < len(blocks):
+                hidden[step] = first_layer(*blocks[step])
+            if 1 <= step <= len(blocks):
+                features[step - 1] = second_layer(hidden.pop(step - 1))
+            if step >= 2:
+                decode(*blocks[step - 2], features.pop(step - 2))
+
+    loads[5].wait()
+    lvr[0, 8:24, :] = pltpu.roll(lv[...], 1, 1)
+    lvr[1, 8:24, :] = lv[...]
+    lvr[2, 8:24, :] = pltpu.roll(lv[...], ncols - 1, 1)
+    for i in range(1, nrows + 1):
+        for t in inner:
+            encode(i, t)
+    network([(g, t) for g in (1, 2) for t in inner])
+    for load in loads[6:]:
+        load.wait()
+    colsb[:, 0:ncols] = cols[...].astype(BF16)
+    share = U // npx
+    er = lax.broadcasted_iota(jnp.int32, (4 * U, U), 0)
+    ec = lax.broadcasted_iota(jnp.int32, (4 * U, U), 1)
+    pick = jnp.where((er // (4 * share)) * share + er % share == ec, 1.0, 0.0).astype(BF16)
+    wr = lax.broadcasted_iota(jnp.int32, (U, U), 0)
+    placed = jnp.where(wr == order[...], 1.0, 0.0).astype(BF16)
+    pick = nt_dot(pick, placed).astype(BF16)
 
     for copy in side_copies:
         copy.wait()
     place(8, lv[...], None)
     for i in range(1, nrows + 1):
-        encode(i)
-    tap = group(1)
-    taps[160:480, :] = tap
-    tap = group(2)
-    taps[320:480, :] += tap[0:160]
-    taps[480:640, :] = tap[160:320]
-    for copy in edge_copies:
-        copy.wait()
-    place(0, lvx[0:8, :], first_up)
-    place(24, lvx[8:16, :], last_down)
-    encode(0)
-    encode(nrows + 1)
-    tap = group(0)
-    taps[0:160, :] = tap[0:160]
-    taps[160:320, :] += tap[160:320]
-    tap = group(3)
-    taps[480:640, :] += tap[0:160]
-    taps[640:800, :] = tap[160:320]
-
+        for t in outer:
+            encode(i, t)
+    network([(g, t) for g in (1, 2) for t in outer])
     for copy in green_copies:
         copy.wait()
     clane = lax.broadcasted_iota(jnp.int32, cols_right.shape, 1)
@@ -221,6 +244,15 @@
             blocks += [own[at : at + 16], mixed[at : at + 16]] * 4
         spread = nt_dot(pick, jnp.concatenate(blocks, axis=0))
         lhs[z] = jnp.where(pr == pc, spread, 0.0).astype(BF16)
+
+    for copy in edge_copies:
+        copy.wait()
+    place(0, lvx[0:8, :], first_up)
+    place(24, lvx[8:16, :], last_down)
+    for i in (0, nrows + 1):
+        for t in range(count):
+            encode(i, t)
+    network([(g, t) for g in (0, 3) for t in range(count)])
 
     blank = jnp.zeros((CH, LANE), F32)
     tiles = []
@@ -357,6 +389,7 @@
             pltpu.VMEM((2 * HID, 192), F32),
             pltpu.VMEM((4 * HID, 4 * HID), F32),
             pltpu.VMEM((8 * KS * CH, 4 * HID), F32),
+            pltpu.VMEM((6 * HID, LANE), F32),
             pltpu.VMEM(((nrows + 2 * M) * KS * CH, ncols), F32),
             pltpu.VMEM(cols.shape, F32),
             pltpu.VMEM((cols.shape[0], LANE), F32),

time: 32.4 us -> 34.3 us (1.059)
  Pallas kernels: 30.9 us -> 32.7 us
    pallas_call x1, Pallas kernels: 30.9 us -> 32.7 us  [on_device(): pl.pallas_call(functools.partial(kernel, npx, npy, scatter), out_shape=ja...]
where the time goes in v3:
time: 34.3 us; the launch traced here: 34.1 us
  Pallas kernels  32.7 us (95%)
  local copies, waits for them, and re-layouts  1.38 us (4%)
    pallas_call x1, Pallas kernels, on_device(): pl.pallas_call(functools.partial(kernel, npx, npy, scatter), out_shape=ja...  32.7 us
    unnamed x1, local copies, waits for them, and re-layouts  1.38 us

profile of v3, /device:TPU:0, one launch (start us, length us, event | category | flops | bytes accessed | tf_op | source)
XLA Modules:
  0.0 34.1 jit_solution(771788456249622890)
XLA Ops:
  0.0 32.7 %shard_map.91 = f32[4,4,512]{2,1,0:T(4,128)} custom-call(s32[16,1024]{1,0:T(8,128)} %lv_in.1, bf16[64,144]{1,0:T(8,128)(2,1)} %table_in.1, f32[1,64]{1,0:T(1,128)} %bitcast.9, bf16[64,64]{1,0:T(8,128)(2,1)} %mix_in.1, f32[1,64]{1,0:T(1,128)} %bitcast.10, bf16[5,40,64]{2,1,0:T(8,128)(2,1)} %dec_in.1, f32[256,64]{1,0:T(8,128)} %bitcast.8, ...), custom_call_target="tpu_custom_call" | custom-call | tf_op jit(solution)/shard_map/pallas_call | solution.py:377
  32.7 1.4 %copy.11 = f32[4,4,512]{2,1,0:T(4,128)} copy(f32[4,4,512]{2,1,0:T(4,128)} %shard_map.91) | data formatting | bytes 65536

commit v4 on v2

--- a/solution.py
+++ b/solution.py
@@ -41,7 +41,7 @@
     lv_in, table_in, cb_in, mix_in, mb_in, dec_in, rows_in, cols_in, order_in, out,
     lv, table, conv_bias, mix, mix_bias, dec, rows, order,
     lvx, lv_right, lv_left, lvr, onehot, w1, w2, wd, taps, cols, cols_right, cols_left, colsb,
-    rows_up, rows_down, lhs, field, r0, a0, r1a, r1b, a1a, a1b, r2a, r2b, a2, r3,
+    rows_up, rows_down, rows_edge, cols_edge, lhs, field, r0, a0, r1a, r1b, a1a, a1b, r2a, r2b, a2, r3,
     send, recv, rs_send, rs_recv, load_sem,
 ):
     px = lax.axis_index("px")
@@ -120,15 +120,31 @@
         remote(6, lv_in.at[0:8, 0:LANE], lv_right.at[24:32, :], (up, left)),
         remote(7, lv_in.at[0:8, last:ncols], lv_left.at[24:32, :], (up, right)),
     ]
-    green_copies = [
-        remote(8, rows_in, rows_up, (down, py)),
-        remote(9, rows_in, rows_down, (up, py)),
-        remote(10, cols_in.at[:, 0:LANE], cols_right, (px, left)),
-        remote(11, cols_in.at[:, last:ncols], cols_left, (px, right)),
-    ]
     for load in loads[5:]:
         load.wait()
     colsb[:, 0:ncols] = cols[...].astype(BF16)
+
+    def grid(shape):
+        return lax.broadcasted_iota(jnp.int32, shape, 0), lax.broadcasted_iota(jnp.int32, shape, 1)
+
+    def mark(where):
+        return jnp.where(where, 1.0, 0.0).astype(BF16)
+
+    own = rows[...].astype(BF16)
+    r, c = grid((2 * 2 * Z, nrows * 2 * Z))
+    near_rows = (c // nrows == r // 2) & (c % nrows == r % 2)
+    far_rows = (c // nrows == r // 2) & (c % nrows == nrows - M + r % 2)
+    rows_edge[0] = jnp.dot(mark(near_rows), own, preferred_element_type=F32)
+    rows_edge[1] = jnp.dot(mark(far_rows), own, preferred_element_type=F32)
+    r, c = grid((16, LANE))
+    cols_edge[0] = nt_dot(mark((r < M) & (c == r)), colsb[:, 0:LANE])[0:8]
+    cols_edge[1] = nt_dot(mark((r < M) & (c == LANE - M + r)), colsb[:, last:ncols])[0:8]
+    green_copies = [
+        remote(8, rows_edge.at[0], rows_down, (up, py)),
+        remote(9, rows_edge.at[1], rows_up, (down, py)),
+        remote(10, cols_edge.at[0], cols_right, (px, left)),
+        remote(11, cols_edge.at[1], cols_left, (px, right)),
+    ]
     share = U // npx
     er = lax.broadcasted_iota(jnp.int32, (4 * U, U), 0)
     ec = lax.broadcasted_iota(jnp.int32, (4 * U, U), 1)
@@ -198,20 +214,20 @@
 
     for copy in green_copies:
         copy.wait()
-    clane = lax.broadcasted_iota(jnp.int32, cols_right.shape, 1)
-    colsb[:, ncols:wide] = jnp.where(
-        clane < 64,
-        jnp.where(last_right, 0.0, cols_right[...]),
-        jnp.where(first_left, 0.0, cols_left[...]),
+    edge = jnp.concatenate(
+        [jnp.where(last_right, 0.0, cols_right[...]), jnp.where(first_left, 0.0, cols_left[...])], axis=0
+    )
+    r, c = grid((16, LANE))
+    target = mark(((r < M) & (c == r)) | ((r >= 8) & (r < 8 + M) & (c == LANE - M - 8 + r)))
+    colsb[:, ncols:wide] = jnp.dot(edge.T.astype(BF16), target, preferred_element_type=F32).astype(BF16)
+
+    edge = jnp.concatenate(
+        [jnp.where(first_up, 0.0, rows_up[...]), jnp.where(last_down, 0.0, rows_down[...])], axis=0
     ).astype(BF16)
-
-    xrow = lax.broadcasted_iota(jnp.int32, rows.shape, 0) % 16
-    mixed = jnp.where(
-        xrow < 8,
-        jnp.where(last_down, 0.0, rows_down[...]),
-        jnp.where(first_up, 0.0, rows_up[...]),
-    ).astype(BF16)
-    own = rows[...].astype(BF16)
+    r, c = grid((nrows * 2 * Z, 4 * 2 * Z))
+    above = (c < 4 * Z) & (r // nrows == c // 2) & (r % nrows == nrows - M + c % 2)
+    below = (c >= 4 * Z) & (r // nrows == c // 2 - 2 * Z) & (r % nrows == c % 2)
+    mixed = jnp.dot(mark(above | below), edge, preferred_element_type=F32).astype(BF16)
     pr = (lax.broadcasted_iota(jnp.int32, (4 * U, 2 * LANE), 0) // share) % 4
     pc = (lax.broadcasted_iota(jnp.int32, (4 * U, 2 * LANE), 1) // 32) % 4
     for z in range(Z):
@@ -359,11 +375,13 @@
             pltpu.VMEM((8 * KS * CH, 4 * HID), F32),
             pltpu.VMEM(((nrows + 2 * M) * KS * CH, ncols), F32),
             pltpu.VMEM(cols.shape, F32),
-            pltpu.VMEM((cols.shape[0], LANE), F32),
-            pltpu.VMEM((cols.shape[0], LANE), F32),
+            pltpu.VMEM((8, cols.shape[0]), F32),
+            pltpu.VMEM((8, cols.shape[0]), F32),
             pltpu.VMEM((cols.shape[0], wide), BF16),
-            like(rows),
-            like(rows),
+            pltpu.VMEM((4 * Z, U), F32),
+            pltpu.VMEM((4 * Z, U), F32),
+            pltpu.VMEM((2, 4 * Z, U), F32),
+            pltpu.VMEM((2, 8, cols.shape[0]), F32),
             pltpu.VMEM((Z, 4 * U, 2 * LANE), BF16),
             rs(2, 2, 4, 2, 2, 16, LANE),
             rs(2, 2, 4, 2, 2, 16, LANE),

time: 32.4 us -> 32.2 us (level)
  no operation moved by 1% of the time
where the time goes in v4:
time: 32.2 us; the launch traced here: 32 us
  Pallas kernels  30.6 us (95%)
  local copies, waits for them, and re-layouts  1.38 us (4%)
    pallas_call x1, Pallas kernels, on_device(): pl.pallas_call(functools.partial(kernel, npx, npy, scatter), out_shape=ja...  30.6 us
    unnamed x1, local copies, waits for them, and re-layouts  1.38 us

profile of v4, /device:TPU:0, one launch (start us, length us, event | category | flops | bytes accessed | tf_op | source)
XLA Modules:
  0.0 32.0 jit_solution(5608474820548922648)
XLA Ops:
  0.0 30.6 %shard_map.91 = f32[4,4,512]{2,1,0:T(4,128)} custom-call(s32[16,1024]{1,0:T(8,128)} %lv_in.1, bf16[64,144]{1,0:T(8,128)(2,1)} %table_in.1, f32[1,64]{1,0:T(1,128)} %bitcast.9, bf16[64,64]{1,0:T(8,128)(2,1)} %mix_in.1, f32[1,64]{1,0:T(1,128)} %bitcast.10, bf16[5,40,64]{2,1,0:T(8,128)(2,1)} %dec_in.1, f32[256,64]{1,0:T(8,128)} %bitcast.8, ...), custom_call_target="tpu_custom_call" | custom-call | tf_op jit(solution)/shard_map/pallas_call | solution.py:361
  30.6 1.4 %copy.11 = f32[4,4,512]{2,1,0:T(4,128)} copy(f32[4,4,512]{2,1,0:T(4,128)} %shard_map.91) | data formatting | bytes 65536

commit v5 on v4

--- a/solution.py
+++ b/solution.py
@@ -41,7 +41,7 @@
     lv_in, table_in, cb_in, mix_in, mb_in, dec_in, rows_in, cols_in, order_in, out,
     lv, table, conv_bias, mix, mix_bias, dec, rows, order,
     lvx, lv_right, lv_left, lvr, onehot, w1, w2, wd, taps, cols, cols_right, cols_left, colsb,
-    rows_up, rows_down, rows_edge, cols_edge, lhs, field, r0, a0, r1a, r1b, a1a, a1b, r2a, r2b, a2, r3,
+    rows_up, rows_down, rows_edge, cols_edge, near_t, lhs, field, r0, a0, r1a, r1b, a1a, a1b, r2a, r2b, a2, r3,
     send, recv, rs_send, rs_recv, load_sem,
 ):
     px = lax.axis_index("px")
@@ -97,6 +97,34 @@
     bias2 = column(0.5 * mix_bias[...])
     bias2 = jnp.concatenate([bias2] * 4, axis=0)
 
+    last = ncols - LANE
+    for load in loads[5:]:
+        load.wait()
+    colsb[:, 0:ncols] = cols[...].astype(BF16)
+
+    def grid(shape):
+        return lax.broadcasted_iota(jnp.int32, shape, 0), lax.broadcasted_iota(jnp.int32, shape, 1)
+
+    def mark(where):
+        return jnp.where(where, 1.0, 0.0).astype(BF16)
+
+    own = rows[...].astype(BF16)
+    r, c = grid((2 * 2 * Z, nrows * 2 * Z))
+    near_rows = (c // nrows == r // 2) & (c % nrows == r % 2)
+    far_rows = (c // nrows == r // 2) & (c % nrows == nrows - M + r % 2)
+    rows_edge[0] = jnp.dot(mark(near_rows), own, preferred_element_type=F32)
+    rows_edge[1] = jnp.dot(mark(far_rows), own, preferred_element_type=F32)
+    r, c = grid((16, LANE))
+    cols_edge[0] = nt_dot(mark((r < M) & (c == r)), colsb[:, 0:LANE])[0:8]
+    cols_edge[1] = nt_dot(mark((r < M) & (c == LANE - M + r)), colsb[:, last:ncols])[0:8]
+    share = U // npx
+    er = lax.broadcasted_iota(jnp.int32, (4 * U, U), 0)
+    ec = lax.broadcasted_iota(jnp.int32, (4 * U, U), 1)
+    pick = jnp.where((er // (4 * share)) * share + er % share == ec, 1.0, 0.0).astype(BF16)
+    wr = lax.broadcasted_iota(jnp.int32, (U, U), 0)
+    placed = jnp.where(wr == order[...], 1.0, 0.0).astype(BF16)
+    pick = nt_dot(pick, placed).astype(BF16)
+
     pl.semaphore_wait(barrier, len(greeted))
 
     def remote(slot, src, dst, device):
@@ -107,7 +135,6 @@
         copy.start()
         return copy
 
-    last = ncols - LANE
     side_copies = [
         remote(0, lv_in.at[:, 0:LANE], lv_right.at[8:24, :], (px, left)),
         remote(1, lv_in.at[:, last:ncols], lv_left.at[8:24, :], (px, right)),
@@ -120,38 +147,12 @@
         remote(6, lv_in.at[0:8, 0:LANE], lv_right.at[24:32, :], (up, left)),
         remote(7, lv_in.at[0:8, last:ncols], lv_left.at[24:32, :], (up, right)),
     ]
-    for load in loads[5:]:
-        load.wait()
-    colsb[:, 0:ncols] = cols[...].astype(BF16)
-
-    def grid(shape):
-        return lax.broadcasted_iota(jnp.int32, shape, 0), lax.broadcasted_iota(jnp.int32, shape, 1)
-
-    def mark(where):
-        return jnp.where(where, 1.0, 0.0).astype(BF16)
-
-    own = rows[...].astype(BF16)
-    r, c = grid((2 * 2 * Z, nrows * 2 * Z))
-    near_rows = (c // nrows == r // 2) & (c % nrows == r % 2)
-    far_rows = (c // nrows == r // 2) & (c % nrows == nrows - M + r % 2)
-    rows_edge[0] = jnp.dot(mark(near_rows), own, preferred_element_type=F32)
-    rows_edge[1] = jnp.dot(mark(far_rows), own, preferred_element_type=F32)
-    r, c = grid((16, LANE))
-    cols_edge[0] = nt_dot(mark((r < M) & (c == r)), colsb[:, 0:LANE])[0:8]
-    cols_edge[1] = nt_dot(mark((r < M) & (c == LANE - M + r)), colsb[:, last:ncols])[0:8]
     green_copies = [
         remote(8, rows_edge.at[0], rows_down, (up, py)),
         remote(9, rows_edge.at[1], rows_up, (down, py)),
         remote(10, cols_edge.at[0], cols_right, (px, left)),
         remote(11, cols_edge.at[1], cols_left, (px, right)),
     ]
-    share = U // npx
-    er = lax.broadcasted_iota(jnp.int32, (4 * U, U), 0)
-    ec = lax.broadcasted_iota(jnp.int32, (4 * U, U), 1)
-    pick = jnp.where((er // (4 * share)) * share + er % share == ec, 1.0, 0.0).astype(BF16)
-    wr = lax.broadcasted_iota(jnp.int32, (U, U), 0)
-    placed = jnp.where(wr == order[...], 1.0, 0.0).astype(BF16)
-    pick = nt_dot(pick, placed).astype(BF16)
 
     first_up, last_down = px == 0, px == npx - 1
     first_left, last_right = py == 0, py == npy - 1
@@ -252,11 +253,11 @@
     pr = lax.broadcasted_iota(jnp.int32, (CH * 32, CH * ext), 0)
     pc = lax.broadcasted_iota(jnp.int32, (CH * 32, CH * ext), 1)
     perm = jnp.where((pr // 32 == pc % 8) & ((pc // 8 + 30) % 32 == pr % 32), 1.0, 0.0).astype(BF16)
-    near_field = jnp.dot(perm, near_field, preferred_element_type=F32).astype(BF16)
+    near_t[...] = jnp.dot(perm, near_field, preferred_element_type=F32).T.astype(BF16)
 
     def planes(c):
         cut = pl.ds(pl.multiple_of(256 * c, 256), 256)
-        sums = nt_dot(colsb[cut, :], near_field)
+        sums = jnp.dot(colsb[cut, :], near_t[...], preferred_element_type=F32)
         fields = []
         for z in range(2):
             one = sums[LANE * z : LANE * z + LANE, 0:LANE]
@@ -269,7 +270,8 @@
             high = value.astype(BF16)
             low = (value - high.astype(F32)).astype(BF16)
             left_side = lhs[2 * c + z]
-            fields.append(nt_dot(left_side, high) + nt_dot(left_side, low))
+            both = nt_dot(left_side, jnp.concatenate([high, low], axis=0))
+            fields.append(both[:, 0:LANE] + both[:, LANE : 2 * LANE])
         return fields
 
     if not scatter:
@@ -382,6 +384,7 @@
             pltpu.VMEM((4 * Z, U), F32),
             pltpu.VMEM((2, 4 * Z, U), F32),
             pltpu.VMEM((2, 8, cols.shape[0]), F32),
+            pltpu.VMEM((wide, CH * 32), BF16),
             pltpu.VMEM((Z, 4 * U, 2 * LANE), BF16),
             rs(2, 2, 4, 2, 2, 16, LANE),
             rs(2, 2, 4, 2, 2, 16, LANE),

time: 32.2 us -> 31.8 us (0.988)
  Pallas kernels: 30.6 us -> 30.2 us
    pallas_call x1, Pallas kernels: 30.6 us -> 30.2 us  [on_device(): pl.pallas_call(functools.partial(kernel, npx, npy, scatter), out_shape=ja...]
where the time goes in v5:
time: 31.8 us; the launch traced here: 31.6 us
  Pallas kernels  30.2 us (95%)
  local copies, waits for them, and re-layouts  1.38 us (4%)
    pallas_call x1, Pallas kernels, on_device(): pl.pallas_call(functools.partial(kernel, npx, npy, scatter), out_shape=ja...  30.2 us
    unnamed x1, local copies, waits for them, and re-layouts  1.38 us

profile of v5, /device:TPU:0, one launch (start us, length us, event | category | flops | bytes accessed | tf_op | source)
XLA Modules:
  0.0 31.6 jit_solution(5277688557270308337)
XLA Ops:
  0.0 30.2 %shard_map.91 = f32[4,4,512]{2,1,0:T(4,128)} custom-call(s32[16,1024]{1,0:T(8,128)} %lv_in.1, bf16[64,144]{1,0:T(8,128)(2,1)} %table_in.1, f32[1,64]{1,0:T(1,128)} %bitcast.9, bf16[64,64]{1,0:T(8,128)(2,1)} %mix_in.1, f32[1,64]{1,0:T(1,128)} %bitcast.10, bf16[5,40,64]{2,1,0:T(8,128)(2,1)} %dec_in.1, f32[256,64]{1,0:T(8,128)} %bitcast.8, ...), custom_call_target="tpu_custom_call" | custom-call | tf_op jit(solution)/shard_map/pallas_call | solution.py:363
  30.2 1.4 %copy.11 = f32[4,4,512]{2,1,0:T(4,128)} copy(f32[4,4,512]{2,1,0:T(4,128)} %shard_map.91) | data formatting | bytes 65536

commit v6 on v5

--- a/solution.py
+++ b/solution.py
@@ -41,7 +41,7 @@
     lv_in, table_in, cb_in, mix_in, mb_in, dec_in, rows_in, cols_in, order_in, out,
     lv, table, conv_bias, mix, mix_bias, dec, rows, order,
     lvx, lv_right, lv_left, lvr, onehot, w1, w2, wd, taps, cols, cols_right, cols_left, colsb,
-    rows_up, rows_down, rows_edge, cols_edge, near_t, lhs, field, r0, a0, r1a, r1b, a1a, a1b, r2a, r2b, a2, r3,
+    rows_up, rows_down, rows_edge, cols_edge, near_t, lhs, field, r0, a0, r1a, r1b, r1h, a1a, a1b, a1h, r2a, r2b, r2h, a2, r3, rz, c1, c2, rcx, rcy,
     send, recv, rs_send, rs_recv, load_sem,
 ):
     px = lax.axis_index("px")
@@ -292,49 +292,78 @@
         for z, value in enumerate(planes(2 * (1 - py) + i)):
             field[i, z] = value.reshape(field.shape[2:])
         core.append(exchange(i, field.at[i], r0.at[i], (px, 1 - py)))
-    step1 = []
-    for i in range(2):
+    def own_planes(i):
         values = planes(2 * py + i)
         core[i].wait()
         for z in range(2):
             a0[i, z] = values[z].reshape(field.shape[2:]) + r0[i, z]
-        step1.append((
-            exchange(2 + 7 * i, a0.at[i, 0, :, :, 1 - xq], r1a.at[i], xdev),
-            exchange(3 + 7 * i, a0.at[i, 1, :, 1 - yq], r1b.at[i], ydev),
-        ))
-    step2 = []
-    for i in range(2):
-        step1[i][0].wait()
-        a1a[i] = a0[i, 0, :, :, xq] + r1a[i]
-        da = exchange(4 + 7 * i, a1a.at[i, :, 1 - yq], r2a.at[i], ydev)
-        step1[i][1].wait()
-        a1b[i] = a0[i, 1, :, yq] + r1b[i]
-        db = exchange(5 + 7 * i, a1b.at[i, :, 1 - xq], r2b.at[i], xdev)
-        step2.append((da, db))
-    step3 = []
-    for i in range(2):
-        step2[i][0].wait()
-        a2[i, :, 0] = a1a[i, :, yq] + r2a[i]
-        step2[i][1].wait()
-        a2[i, :, 1] = a1b[i, :, xq] + r2b[i]
-        step3.append([
-            exchange(6 + 7 * i + d, a2.at[i, lax.rem(zq + d + 1, 4)], r3.at[i, d], zdevs[d])
+
+    own_planes(0)
+    step_a = exchange(2, a0.at[0, 0, :, :, 1 - xq], r1a, xdev)
+    step_c = [
+        exchange(3 + d, a0.at[0, 1, lax.rem(zq + d + 1, 4)], rz.at[d], zdevs[d]) for d in range(3)
+    ]
+    own_planes(1)
+    step_b = exchange(6, a0.at[1, 0, :, 1 - yq], r1b, ydev)
+    step_g = exchange(7, a0.at[1, 1, :, :, 1 - xq, 0:8], r1h.at[0], xdev)
+    step_h = exchange(8, a0.at[1, 1, :, 1 - yq, :, 8:16], r1h.at[1], ydev)
+    step_a.wait()
+    a1a[...] = a0[0, 0, :, :, xq] + r1a[...]
+    step_a = exchange(9, a1a.at[:, 1 - yq], r2a, ydev)
+    step_b.wait()
+    a1b[...] = a0[1, 0, :, yq] + r1b[...]
+    step_b = exchange(10, a1b.at[:, 1 - xq], r2b, xdev)
+    step_g.wait()
+    a1h[0] = a0[1, 1, :, :, xq, 0:8] + r1h[0]
+    step_g = exchange(11, a1h.at[0, :, 1 - yq], r2h.at[0], ydev)
+    step_h.wait()
+    a1h[1] = a0[1, 1, :, yq, :, 8:16] + r1h[1]
+    step_h = exchange(12, a1h.at[1, :, 1 - xq], r2h.at[1], xdev)
+
+    def last_step(k):
+        return [
+            exchange(15 + 3 * k + d, a2.at[k, lax.rem(zq + d + 1, 4)], r3.at[k, d], zdevs[d])
             for d in range(3)
-        ])
+        ]
+
+    total = a0[0, 1, zq]
+    for d, copy in enumerate(step_c):
+        copy.wait()
+        total = total + rz[d]
+    c1[...] = total
+    step_c = exchange(13, c1.at[:, 1 - xq], rcx, xdev)
+    step_a.wait()
+    a2[0] = a1a[:, yq] + r2a[...]
+    ends = [last_step(0)]
+    step_b.wait()
+    a2[1] = a1b[:, xq] + r2b[...]
+    ends.append(last_step(1))
+    step_g.wait()
+    a2[2, :, 0:8] = a1h[0, :, yq] + r2h[0]
+    step_h.wait()
+    a2[2, :, 8:16] = a1h[1, :, xq] + r2h[1]
+    ends.append(last_step(2))
+    step_c.wait()
+    c2[...] = c1[:, xq] + rcx[...]
+    step_c = exchange(14, c2.at[1 - yq], rcy, ydev)
+    results = []
+    for k in range(3):
+        total = a2[k, zq]
+        for d, copy in enumerate(ends[k]):
+            copy.wait()
+            total = total + r3[k, d]
+        results.append(total)
+    step_c.wait()
+    results.insert(1, c2[yq] + rcy[...])
     first_half = lax.broadcasted_iota(jnp.int32, (share, LANE), 1) < 64
-    for i in range(2):
-        result = a2[i, zq]
-        for d, copy in enumerate(step3[i]):
-            copy.wait()
-            result = result + r3[i, d]
-        for z in range(2):
-            reals, imags = [], []
-            for j in range(2):
-                even = result[z, 2 * j * share : (2 * j + 1) * share]
-                odd = result[z, (2 * j + 1) * share : (2 * j + 2) * share]
-                reals.append(jnp.where(first_half, even, pltpu.roll(odd, 64, 1)))
-                imags.append(jnp.where(first_half, pltpu.roll(even, 64, 1), odd))
-            out[2 * i + z] = jnp.concatenate(reals + imags, axis=1)
+    for z, result in enumerate(results):
+        reals, imags = [], []
+        for j in range(2):
+            even = result[2 * j * share : (2 * j + 1) * share]
+            odd = result[(2 * j + 1) * share : (2 * j + 2) * share]
+            reals.append(jnp.where(first_half, even, pltpu.roll(odd, 64, 1)))
+            imags.append(jnp.where(first_half, pltpu.roll(even, 64, 1), odd))
+        out[z] = jnp.concatenate(reals + imags, axis=1)
 
 
 def on_device(
@@ -389,18 +418,26 @@
             rs(2, 2, 4, 2, 2, 16, LANE),
             rs(2, 2, 4, 2, 2, 16, LANE),
             rs(2, 2, 4, 2, 2, 16, LANE),
-            rs(2, 4, 2, 16, LANE),
-            rs(2, 4, 2, 16, LANE),
-            rs(2, 4, 2, 16, LANE),
-            rs(2, 4, 2, 16, LANE),
-            rs(2, 4, 16, LANE),
-            rs(2, 4, 16, LANE),
-            rs(2, 4, 2, 16, LANE),
-            rs(2, 3, 2, 16, LANE),
+            rs(4, 2, 16, LANE),
+            rs(4, 2, 16, LANE),
+            rs(2, 4, 2, 8, LANE),
+            rs(4, 2, 16, LANE),
+            rs(4, 2, 16, LANE),
+            rs(2, 4, 2, 8, LANE),
+            rs(4, 16, LANE),
+            rs(4, 16, LANE),
+            rs(2, 4, 8, LANE),
+            rs(3, 4, 16, LANE),
+            rs(3, 3, 16, LANE),
+            rs(3, 2, 2, 16, LANE),
+            rs(2, 2, 16, LANE),
+            rs(2, 16, LANE),
+            rs(2, 16, LANE),
+            rs(16, LANE),
             pltpu.SemaphoreType.DMA((12,)),
             pltpu.SemaphoreType.DMA((12,)),
-            pltpu.SemaphoreType.DMA((16,)),
-            pltpu.SemaphoreType.DMA((16,)),
+            pltpu.SemaphoreType.DMA((24,)),
+            pltpu.SemaphoreType.DMA((24,)),
             pltpu.SemaphoreType.DMA((9,)),
         ],
         compiler_params=pltpu.CompilerParams(

time: 31.8 us -> 31.9 us (level)
  no operation moved by 1% of the time
where the time goes in v6:
time: 31.9 us; the launch traced here: 31.7 us
  Pallas kernels  30.3 us (95%)
  local copies, waits for them, and re-layouts  1.38 us (4%)
    pallas_call x1, Pallas kernels, on_device(): pl.pallas_call(functools.partial(kernel, npx, npy, scatter), out_shape=ja...  30.3 us
    unnamed x1, local copies, waits for them, and re-layouts  1.38 us

profile of v6, /device:TPU:0, one launch (start us, length us, event | category | flops | bytes accessed | tf_op | source)
XLA Modules:
  0.0 31.7 jit_solution(6423987762622355536)
XLA Ops:
  0.0 30.3 %shard_map.91 = f32[4,4,512]{2,1,0:T(4,128)} custom-call(s32[16,1024]{1,0:T(8,128)} %lv_in.1, bf16[64,144]{1,0:T(8,128)(2,1)} %table_in.1, f32[1,64]{1,0:T(1,128)} %bitcast.9, bf16[64,64]{1,0:T(8,128)(2,1)} %mix_in.1, f32[1,64]{1,0:T(1,128)} %bitcast.10, bf16[5,40,64]{2,1,0:T(8,128)(2,1)} %dec_in.1, f32[256,64]{1,0:T(8,128)} %bitcast.8, ...), custom_call_target="tpu_custom_call" | custom-call | tf_op jit(solution)/shard_map/pallas_call | solution.py:392
  30.3 1.4 %copy.11 = f32[4,4,512]{2,1,0:T(4,128)} copy(f32[4,4,512]{2,1,0:T(4,128)} %shard_map.91) | data formatting | bytes 65536
